TPU v7x, 512 devices: a whole 4x8x8 slice. The times are simulated.
512 devices in a mesh: group: 8 (over y_lo, core), blk: 64 (over x, z, y_hi).
Axes of the slice: x: 4, y: 8 (y_hi: 2, y_lo: 4; y = y_hi * 4 + y_lo), z: 8, core: 2. Of those that a mesh axis runs over, the one named last changes fastest.
Arguments:
- picture_vectors: bfloat16 [65536, 1152], P(('group', 'blk')), may hold values from -1 to 1
- caption_vectors: bfloat16 [65536, 1152], P(('group', 'blk')), may hold values from -1 to 1
- inverse_heat_factor: float32 [1], replicated, may hold values from 0.5 to 2
- score_shift_term: float32 [1], replicated, may hold values from -3 to 1
Outputs:
- grad_images: float32 [65536, 1152], P(('group', 'blk'))
- grad_texts: float32 [65536, 1152], P(('group', 'blk'))
- row_loss: float32 [65536], P(('group', 'blk'))
All inputs are finite; a program needn't handle non-finite values.
Results may differ from a plain program's by a relative error of at most 0.015.
Values may be sent and summed in bfloat16 or wider, within the bound.
No kernel may reach another device: no remote copies, remote signals or barrier semaphores. Data moves between devices by JAX's collectives and lax.ppermute only.
A program may use at most 64 MiB of HBM per device.

v0:
```python
import jax
import jax.numpy as jnp
from jax import lax
from jax.sharding import PartitionSpec as P

SPAN = 2


def passed_along(array, axis, by):
    length = lax.axis_size(axis)
    return lax.ppermute(array, axis, [(i, (i + by) % length) for i in range(length)])


def contract_rows(left, right):
    return lax.dot_general(
        left, right, (((1,), (1,)), ((), ())), preferred_element_type=jnp.float32
    )


def contract_first(left, right):
    return lax.dot_general(
        left, right, (((0,), (0,)), ((), ())), preferred_element_type=jnp.float32
    )


def tile_terms(picture_vectors, text_bundle, positives, step, score_multiplier, shift_value):
    scaled = score_multiplier * contract_rows(picture_vectors, text_bundle) + shift_value
    if step == 0:
        signs = jnp.where(positives, 1.0, -1.0).astype(jnp.float32)
    else:
        signs = -jnp.ones_like(scaled)
    objective_piece = jnp.sum(jax.nn.softplus(-signs * scaled), axis=1)
    slopes = (-signs * jax.nn.sigmoid(-signs * scaled) * score_multiplier).astype(jnp.bfloat16)
    return (objective_piece, slopes)


def shards(picture_vectors, caption_vectors, inverse_heat_factor, score_shift_term):
    group_width = lax.axis_size("group")
    group_index = lax.axis_index("group")
    row_count = picture_vectors.shape[0]
    bundle_rows = row_count * group_width
    score_multiplier = inverse_heat_factor[0]
    shift_value = score_shift_term[0]
    text_bundle = lax.all_gather(caption_vectors, "group", axis=0, tiled=True)
    positives = (
        jnp.arange(bundle_rows)[None, :] == group_index * row_count + jnp.arange(row_count)[:, None]
    )
    loss_sum = jnp.zeros((row_count,), jnp.float32)
    grad_image = jnp.zeros(picture_vectors.shape, jnp.float32)
    carried_state = jnp.zeros((bundle_rows, picture_vectors.shape[1]), jnp.float32)
    for step in range(SPAN):
        objective_piece, slopes = tile_terms(
            picture_vectors, text_bundle, positives, step, score_multiplier, shift_value
        )
        loss_sum = loss_sum + objective_piece
        grad_image = grad_image + jnp.dot(slopes, text_bundle, preferred_element_type=jnp.float32)
        partial_value = contract_first(slopes, picture_vectors)
        carried_state = carried_state + partial_value
        if step + 1 < SPAN:
            carried_state = passed_along(carried_state.astype(jnp.bfloat16), "blk", 1).astype(
                carried_state.dtype
            )
        if step + 1 < SPAN:
            text_bundle = passed_along(text_bundle, "blk", 1)
    returned = passed_along(carried_state.astype(jnp.bfloat16), "blk", -(SPAN - 1)).astype(
        carried_state.dtype
    )
    grad_text = lax.psum_scatter(
        returned.astype(jnp.bfloat16), "group", scatter_dimension=0, tiled=True
    ).astype(jnp.float32)
    row_loss = loss_sum / (SPAN * bundle_rows)
    return (grad_image, grad_text, row_loss)


def solution(mesh):
    placed = (P(("group", "blk"), None), P(("group", "blk"), None), P(), P())
    return jax.shard_map(
        shards,
        mesh=mesh,
        in_specs=placed,
        out_specs=(P(("group", "blk"), None), P(("group", "blk"), None), P(("group", "blk"))),
        check_vma=False,
    )
```

profile of v0, /device:TPU:61, one launch (start us, length us, event | category | flops | bytes accessed | tf_op | source)
XLA Modules:
  0.0 424.0 jit_solution(13967874328467189994)
XLA Ops:
  7.2 0.0 copy-start
  7.2 0.0 all-gather.2.cloned.1.call-start
  7.2 0.7 all-gather.2.cloned.1.call-update
  7.9 0.0 reduce-scatter.2.cloned.1.call-start
  9.3 47.8 %all-gather.2.cloned.1.call-done = bf16[1024,1152]{1,0:T(8,128)(2,1)} async-done(((bf16[128,1152]{1,0:T(8,128)(2,1)}), bf16[1024,1152]{1,0:T(8,128)(2,1)}) %all-gather.2.cloned.1.call-update) | async-done | bytes 2359312 | tf_op jit(solution)/shard_map/all_gather | solution.py:44
  57.1 4.8 %collective-permute-start = (bf16[1024,1152]{1,0:T(8,128)(2,1)}, bf16[1024,1152]{1,0:T(8,128)(2,1)S(1)}, u32[]{:S(2)}, u32[]{:S(2)}) collective-permute-start(bf16[1024,1152]{1,0:T(8,128)(2,1)} %all-gather.2.cloned.1.call-done), channel_id=1, source_target_pairs={{0,1},{1,2},{2,3},{3,4},{4,5},{5,6},{6,7},{7,8},{8,9},{9,10},{10,1... | collective-permute-start | bytes 7077896 | tf_op jit(solution)/shard_map/ppermute | solution.py:11
  61.9 2.9 fusion.3
  64.8 0.8 copy-done.4
  65.5 0.9 convolution_convert_fusion
  66.5 5.5 %collective-permute-start.1 = (bf16[1024,1152]{1,0:T(8,128)(2,1)S(1)}, bf16[1024,1152]{1,0:T(8,128)(2,1)S(1)}, u32[]{:S(2)}, u32[]{:S(2)}) collective-permute-start(bf16[1024,1152]{1,0:T(8,128)(2,1)S(1)} %convolution_convert_fusion), channel_id=1, source_target_pairs={{0,1},{1,2},{2,3},{3,4},{4,5},{5,6},{6,7},{7,8},{8,9},{9,10},{10,1... | collective-permute-start | bytes 7077896 | tf_op jit(solution)/shard_map/ppermute | solution.py:11
  72.0 143.2 %collective-permute-done = bf16[1024,1152]{1,0:T(8,128)(2,1)S(1)} collective-permute-done((bf16[1024,1152]{1,0:T(8,128)(2,1)}, bf16[1024,1152]{1,0:T(8,128)(2,1)S(1)}, u32[]{:S(2)}, u32[]{:S(2)}) %collective-permute-start) | collective-permute-done | bytes 2359328 | tf_op jit(solution)/shard_map/ppermute | solution.py:11
  215.1 1.1 fusion.4
  216.3 49.9 %collective-permute-done.1 = bf16[1024,1152]{1,0:T(8,128)(2,1)S(1)} collective-permute-done((bf16[1024,1152]{1,0:T(8,128)(2,1)S(1)}, bf16[1024,1152]{1,0:T(8,128)(2,1)S(1)}, u32[]{:S(2)}, u32[]{:S(2)}) %collective-permute-start.1) | collective-permute-done | bytes 2359328 | tf_op jit(solution)/shard_map/ppermute | solution.py:11
  266.2 0.0 copy-done.2
  266.2 0.8 add_convert_fusion
  267.0 8.1 %collective-permute-start.2 = (bf16[1024,1152]{1,0:T(8,128)(2,1)S(1)}, bf16[1024,1152]{1,0:T(8,128)(2,1)S(1)}, u32[]{:S(2)}, u32[]{:S(2)}) collective-permute-start(bf16[1024,1152]{1,0:T(8,128)(2,1)S(1)} %add_convert_fusion), channel_id=1, source_target_pairs={{0,63},{1,0},{2,1},{3,2},{4,3},{5,4},{6,5},{7,6},{8,7},{9,8},{10,9... | collective-permute-start | bytes 7077896 | tf_op jit(solution)/shard_map/ppermute | solution.py:11
  275.1 94.0 %collective-permute-done.2 = bf16[1024,1152]{1,0:T(8,128)(2,1)S(1)} collective-permute-done((bf16[1024,1152]{1,0:T(8,128)(2,1)S(1)}, bf16[1024,1152]{1,0:T(8,128)(2,1)S(1)}, u32[]{:S(2)}, u32[]{:S(2)}) %collective-permute-start.2) | collective-permute-done | bytes 2359328 | tf_op jit(solution)/shard_map/ppermute | solution.py:11
  369.1 1.4 copy-done.1
  370.5 0.0 reduce-scatter.2.cloned.1.call-update
  370.6 2.6 fusion.6
  373.1 0.5 add_multiply_fusion
  373.7 1.4 convolution_add_fusion
  375.0 40.3 %reduce-scatter.2.cloned.1.call-done = bf16[128,1152]{1,0:T(8,128)(2,1)} async-done(((bf16[1024,1152]{1,0:T(8,128)(2,1)}), bf16[128,1152]{1,0:T(8,128)(2,1)}) %reduce-scatter.2.cloned.1.call-update) | async-done | bytes 294928 | tf_op jit(solution)/shard_map/reduce_scatter | solution.py:68
  415.4 1.8 convert_element_type.25
  (7 shorter events, 0.0 us)
Async XLA Ops:
  7.2 54.7 %copy-start = (bf16[128,1152]{1,0:T(8,128)(2,1)S(1)}, bf16[128,1152]{1,0:T(8,128)(2,1)}, u32[]{:S(2)}) copy-start(bf16[128,1152]{1,0:T(8,128)(2,1)} %param.4) | copy-start | bytes 884740
  7.2 49.9 %all-gather.2.cloned.1.call-start = ((), (), s32[]{:S(2)}) async-start(), calls=%async_computation.1 | async-start | bytes 2654208 | tf_op jit(solution)/shard_map/all_gather | solution.py:44
  7.9 407.5 %reduce-scatter.2.cloned.1.call-start = ((), (), s32[]{:S(2)}) async-start(), calls=%async_computation.2 | async-start | bytes 2654208 | tf_op jit(solution)/shard_map/reduce_scatter | solution.py:68
  57.1 158.0 %collective-permute-start = (bf16[1024,1152]{1,0:T(8,128)(2,1)}, bf16[1024,1152]{1,0:T(8,128)(2,1)S(1)}, u32[]{:S(2)}, u32[]{:S(2)}) collective-permute-start(bf16[1024,1152]{1,0:T(8,128)(2,1)} %all-gather.2.cloned.1.call-done), channel_id=1, source_target_pairs={{0,1},{1,2},{2,3},{3,4},{4,5},{5,6},{6,7},{7,8},{8,9},{9,10},{10,1... | collective-permute-start | bytes 7077896 | tf_op jit(solution)/shard_map/ppermute | solution.py:11
  64.8 0.8 copy-start.4
  66.5 199.7 %collective-permute-start.1 = (bf16[1024,1152]{1,0:T(8,128)(2,1)S(1)}, bf16[1024,1152]{1,0:T(8,128)(2,1)S(1)}, u32[]{:S(2)}, u32[]{:S(2)}) collective-permute-start(bf16[1024,1152]{1,0:T(8,128)(2,1)S(1)} %convolution_convert_fusion), channel_id=1, source_target_pairs={{0,1},{1,2},{2,3},{3,4},{4,5},{5,6},{6,7},{7,8},{8,9},{9,10},{10,1... | collective-permute-start | bytes 7077896 | tf_op jit(solution)/shard_map/ppermute | solution.py:11
  215.1 51.0 %copy-start.2 = (bf16[1024,1152]{1,0:T(8,128)(2,1)}, bf16[1024,1152]{1,0:T(8,128)(2,1)S(1)}, u32[]{:S(2)}) copy-start(bf16[1024,1152]{1,0:T(8,128)(2,1)S(1)} %collective-permute-done) | copy-start | bytes 7077892
  267.0 102.1 %collective-permute-start.2 = (bf16[1024,1152]{1,0:T(8,128)(2,1)S(1)}, bf16[1024,1152]{1,0:T(8,128)(2,1)S(1)}, u32[]{:S(2)}, u32[]{:S(2)}) collective-permute-start(bf16[1024,1152]{1,0:T(8,128)(2,1)S(1)} %add_convert_fusion), channel_id=1, source_target_pairs={{0,63},{1,0},{2,1},{3,2},{4,3},{5,4},{6,5},{7,6},{8,7},{9,8},{10,9... | collective-permute-start | bytes 7077896 | tf_op jit(solution)/shard_map/ppermute | solution.py:11
  369.1 1.4 copy-start.1
  370.6 3.1 copy-start.3
Sparse Core Ops, SparseCore 0:
  10.1 46.9 all-gather.1
  370.7 44.6 reduce-scatter.1
where the time goes:
time: 424 us
  waiting for transfers between devices  376 us (89%)
  starting transfers between devices  18.4 us (4%)
  between operations  15.4 us (4%)
  matrix products  9.68 us (2%)
    ppermute x3, waiting for transfers between devices, passed_along(): lax.ppermute(array, axis, [(i, (i + by) % length) for i in range(length)])  287 us
    all_gather x1, waiting for transfers between devices, shards(): text_bundle = lax.all_gather(caption_vectors, 'group', axis=0, tiled=True)  47.8 us
    reduce_scatter x1, waiting for transfers between devices, shards(): lax.psum_scatter(returned.astype(jnp.bfloat16), 'group', scatter_dimensio...  40.3 us
    ppermute x3, starting transfers between devices, passed_along(): lax.ppermute(array, axis, [(i, (i + by) % length) for i in range(length)])  18.4 us
  transfers between devices with their start and end apart: 5, of which 5 were waited for; matrix products, arithmetic and copies ran while one was open for 2% of the time, Pallas kernels for 0%

commit v1 on v0

v1 whole, which is shorter than its diff:
```python
import jax
import jax.numpy as jnp
import numpy as np
from jax import lax
from jax.sharding import Mesh, PartitionSpec as P

AXES = ("yl", "c", "x", "z", "yh")
BF = jnp.bfloat16
F32 = jnp.float32


def pairs(sizes, fn):
    out = []
    for src in np.ndindex(*sizes):
        out.append((int(np.ravel_multi_index(src, sizes)), int(np.ravel_multi_index(fn(*src), sizes))))
    return out


def visit(sizes):
    nyl, _, nx, nz, _ = sizes

    def fn(yl, c, x, z, yh):
        if yh == 1:
            return nyl - 1 - yl, c, x, z, 0
        k = (x * nz + z - 1) % (nx * nz)
        return nyl - 1 - yl, c, k // nz, k % nz, 1

    return pairs(sizes, fn)


def other_core(sizes):
    return pairs(sizes, lambda yl, c, x, z, yh: (yl, 1 - c, x, z, yh))


def contract(left, right, dims):
    return lax.dot_general(left, right, (dims, ((), ())), preferred_element_type=F32)


def split16(v):
    hi = v.astype(BF)
    return hi, (v - hi.astype(F32)).astype(BF)


def pack(rows, values):
    hi, lo = split16(values)
    n, width = values.shape[0], rows.shape[1]
    extra = jnp.zeros((16, width), BF).at[0, :n].set(hi).at[1, :n].set(lo)
    return jnp.concatenate([rows, extra], axis=0)


def unpack(message, n):
    m = message.shape[0] - 16
    values = message[m, :n].astype(F32) + message[m + 1, :n].astype(F32)
    return message[:m].astype(F32), values


def solution(mesh):
    sizes = (4, 2, 4, 8, 2)
    fine = Mesh(mesh.devices.reshape(sizes), AXES)
    go = visit(sizes)
    back = [(b, a) for a, b in go]
    swap = other_core(sizes)

    def shards(images, texts, scale, shift):
        rows, width = images.shape
        yl, c = lax.axis_index("yl"), lax.axis_index("c")
        s, b = scale[0], shift[0]
        visitors = lax.ppermute(images, AXES, go)
        spread = jnp.broadcast_to(texts[None], (4, rows, width))
        bundle = lax.all_to_all(spread, "yl", 0, 0).reshape(4 * rows, width)
        mine = lax.all_gather(images, "c", axis=0, tiled=True)
        theirs = lax.all_gather(visitors, "c", axis=0, tiled=True)
        everyone = jnp.concatenate([mine, theirs], axis=0)
        z = s * contract(everyone, bundle, ((1,), (1,))) + b
        i = lax.broadcasted_iota(jnp.int32, z.shape, 0)
        j = lax.broadcasted_iota(jnp.int32, z.shape, 1)
        positive = (i - c * rows == j - yl * rows) & (i >= c * rows) & (i < (c + 1) * rows)
        u = jnp.where(positive, -z, z)
        e = jnp.exp(-jnp.abs(u))
        loss = jnp.sum(jnp.maximum(u, 0.0) + jnp.log1p(e), axis=1)
        sig = jnp.where(u >= 0, 1.0, e) / (1.0 + e)
        slopes = (jnp.where(positive, -s, s) * sig).astype(BF)
        grad_all = contract(slopes, bundle, ((1,), (0,))).reshape(2, 2, rows, width)
        loss_all = loss.reshape(2, 2, rows)
        keep = lax.dynamic_index_in_dim(grad_all, c, 1, keepdims=False)
        give = lax.dynamic_index_in_dim(grad_all, 1 - c, 1, keepdims=False)
        keep_loss = lax.dynamic_index_in_dim(loss_all, c, 1, keepdims=False)
        give_loss = lax.dynamic_index_in_dim(loss_all, 1 - c, 1, keepdims=False)
        got, got_loss = unpack(
            lax.ppermute(pack(give.reshape(2 * rows, width).astype(BF), give_loss.reshape(-1)), AXES, swap),
            2 * rows,
        )
        grad = keep + got.reshape(2, rows, width)
        loss2 = keep_loss + got_loss.reshape(2, rows)
        home, home_loss = unpack(
            lax.ppermute(pack(grad[1].astype(BF), loss2[1]), AXES, back), rows
        )
        part = contract(slopes, everyone, ((0,), (0,))).astype(BF).reshape(4, rows, width)
        parts = lax.all_to_all(part, "yl", 0, 0)
        grad_texts = jnp.sum(parts.astype(F32), axis=0)
        grad_images = grad[0] + home
        row_loss = (loss2[0] + home_loss) / (16 * rows)
        return grad_images, grad_texts, row_loss

    whole = P(AXES, None)
    return jax.shard_map(
        shards,
        mesh=fine,
        in_specs=(whole, whole, P(), P()),
        out_specs=(whole, whole, P(AXES)),
        check_vma=False,
    )
```

time: 424 us -> 94.4 us (0.22)
  the two profiles are of different devices: /device:TPU:61 before, /device:TPU:8 now
where the time goes in v1:
time: 94.4 us; the launch traced here: 93.9 us
  waiting for transfers between devices  37.9 us (40%)
  starting transfers between devices  32.6 us (35%)
  matrix products  6.1 us (6%)
  other arithmetic  5.72 us (6%)
  local copies, waits for them, and re-layouts  5.03 us (5%)
  blocking collectives  4.44 us (5%)
  between operations  2.14 us (2%)
    ppermute x1, waiting for transfers between devices, shards(): lax.ppermute(pack(grad[1].astype(BF), loss2[1]), AXES, back)  30.9 us
    ppermute x1, starting transfers between devices, shards(): visitors = lax.ppermute(images, AXES, go)  13 us
    all_to_all x1, starting transfers between devices, shards(): bundle = lax.all_to_all(spread, 'yl', 0, 0).reshape(4 * rows, width)  9.45 us
    ppermute x1, waiting for transfers between devices, shards(): visitors = lax.ppermute(images, AXES, go)  6.99 us
    dot_general x3, matrix products, contract(): lax.dot_general(left, right, (dims, ((), ())), preferred_element_type=F32)  6.1 us
    all_to_all x1, starting transfers between devices, shards(): parts = lax.all_to_all(part, 'yl', 0, 0)  5.27 us
    ppermute x1, starting transfers between devices, shards(): lax.ppermute(pack(grad[1].astype(BF), loss2[1]), AXES, back)  2.79 us
    all_gather x1, blocking collectives, shards(): mine = lax.all_gather(images, 'c', axis=0, tiled=True)  2.23 us
  transfers between devices with their start and end apart: 5, of which 2 were waited for; matrix products, arithmetic and copies ran while one was open for 10% of the time, Pallas kernels for 0%

profile of v1, /device:TPU:8, one launch (start us, length us, event | category | flops | bytes accessed | tf_op | source)
XLA Modules:
  0.0 93.9 jit_solution(2834324583134451742)
XLA Ops:
  0.6 2.1 %broadcast_in_dim.20 = bf16[4,128,1152]{2,1,0:T(8,128)(2,1)} broadcast(bf16[128,1152]{1,0:T(8,128)(2,1)} %param.13), dimensions={1,2} | broadcast | bytes 1474560 | tf_op jit(solution)/shard_map/broadcast_in_dim | solution.py:69
  2.7 9.4 %all-to-all-start = ((bf16[4,128,1152]{2,1,0:T(8,128)(2,1)}), bf16[4,128,1152]{2,1,0:T(8,128)(2,1)S(1)}, u32[]{:S(2)}, u32[]{:S(2)}) async-start(bf16[4,128,1152]{2,1,0:T(8,128)(2,1)} %broadcast_in_dim.20), calls=%async_computation | async-start | bytes 2359296 | tf_op jit(solution)/shard_map/all_to_all | solution.py:70
  12.2 13.0 %collective-permute-start = (bf16[128,1152]{1,0:T(8,128)(2,1)S(1)}, bf16[128,1152]{1,0:T(8,128)(2,1)S(1)}, u32[]{:S(2)}, u32[]{:S(2)}) collective-permute-start(bf16[128,1152]{1,0:T(8,128)(2,1)S(1)} %copy-done.3), channel_id=1, source_target_pairs={{0,447},{1,384},{2,385},{3,386},{4,387},{5,388},{6,389},{7,390},{8... | collective-permute-start | bytes 884744 | tf_op jit(solution)/shard_map/ppermute | solution.py:68
  25.2 2.2 %all_gather.6 = bf16[256,1152]{1,0:T(8,128)(2,1)S(1)} all-gather(bf16[128,1152]{1,0:T(8,128)(2,1)S(1)} %copy-done.3), channel_id=1, replica_groups=mesh['yl'=4,'c'=2,'x'=4,'z'=8,'yh'=2] {'c'}, dimensions={0}, use_global_device_ids=true | all-gather | bytes 884736 | tf_op jit(solution)/shard_map/all_gather | solution.py:71
  27.4 0.5 iota_compare_fusion
  29.3 7.0 %collective-permute-done = bf16[128,1152]{1,0:T(8,128)(2,1)S(1)} collective-permute-done((bf16[128,1152]{1,0:T(8,128)(2,1)S(1)}, bf16[128,1152]{1,0:T(8,128)(2,1)S(1)}, u32[]{:S(2)}, u32[]{:S(2)}) %collective-permute-start) | collective-permute-done | bytes 294944 | tf_op jit(solution)/shard_map/ppermute | solution.py:68
  36.3 2.2 %all_gather.7 = bf16[256,1152]{1,0:T(8,128)(2,1)S(1)} all-gather(bf16[128,1152]{1,0:T(8,128)(2,1)S(1)} %collective-permute-done), channel_id=1, replica_groups=mesh['yl'=4,'c'=2,'x'=4,'z'=8,'yh'=2] {'c'}, dimensions={0}, use_global_device_ids=true | all-gather | bytes 884736 | tf_op jit(solution)/shard_map/all_gather | solution.py:72
  38.6 2.1 %multiply_convert_fusion = (bf16[512,512]{1,0:T(8,128)(2,1)S(1)}, f32[512]{0:T(512)S(1)}) fusion(f32[]{:T(128)} %bitcast.39, f32[]{:T(128)S(6)} %neg.9, s32[512]{0:T(512)S(1)} %get-tuple-element.55, s32[512]{0:T(512)S(1)} %get-tuple-element.56, pred[512]{0:T(512)(128)(4,1)S(1)} %get-tuple-element.53, pred[512]{0:T(512)(128)(4,1)S(1)} %copy-done.5, ...), kind=kOutput, calls=%fused_computation.8 | convolution fusion | flops 608960000 | bytes 2890764 | tf_op jit(solution)/shard_map/dot_general | solution.py:36
  40.8 0.9 fusion.7
  41.7 0.2 scatter.15
  42.0 0.9 pad_maximum_fusion
  42.9 2.0 %collective-permute-start.1 = (bf16[272,1152]{1,0:T(8,128)(2,1)}, bf16[272,1152]{1,0:T(8,128)(2,1)}, u32[]{:S(2)}, u32[]{:S(2)}) collective-permute-start(bf16[272,1152]{1,0:T(8,128)(2,1)} %pad_maximum_fusion), channel_id=1, source_target_pairs={{0,64},{1,65},{2,66},{3,67},{4,68},{5,69},{6,70},{7,71},{8,72},{9,... | collective-permute-start | bytes 1880072 | tf_op jit(solution)/shard_map/ppermute | solution.py:90
  44.9 3.2 %convolution_convert_fusion = bf16[512,1152]{1,0:T(8,128)(2,1)} fusion(bf16[512,512]{1,0:T(8,128)(2,1)S(1)} %copy-done.2, bf16[512,1152]{1,0:T(8,128)(2,1)} %copy-done.4), kind=kOutput, calls=%fused_computation | convolution fusion | flops 604569600 | bytes 2883584 | tf_op jit(solution)/shard_map/dot_general | solution.py:36
  48.1 5.3 %all-to-all-start.1 = ((bf16[4,128,1152]{2,1,0:T(8,128)(2,1)}), bf16[4,128,1152]{2,1,0:T(8,128)(2,1)S(1)}, u32[]{:S(2)}, u32[]{:S(2)}) async-start(bf16[4,128,1152]{2,1,0:T(8,128)(2,1)} %bitcast.45), calls=%async_computation.1 | async-start | bytes 2359296 | tf_op jit(solution)/shard_map/all_to_all | solution.py:99
  53.4 0.8 fusion.3
  54.2 1.1 %slice.109 = bf16[256,1152]{1,0:T(8,128)(2,1)S(1)} slice(bf16[272,1152]{1,0:T(8,128)(2,1)} %collective-permute-done.1), slice={[0:256], [0:1152]} | slice | bytes 1179648 | tf_op jit(solution)/shard_map/slice | solution.py:54
  55.3 1.1 %convert_add_fusion = f32[2,128,1152]{2,1,0:T(8,128)} fusion(bf16[2,128,1152]{2,1,0:T(8,128)(2,1)S(1)} %bitcast.44, f32[2,2,128,1152]{3,2,1,0:T(8,128)S(1)} %fusion.7, s32[]{:T(128)S(6)} %select_n.25), kind=kLoop, calls=%fused_computation.5 | loop fusion | flops 589824 | bytes 2949124 | tf_op jit(solution)/shard_map/add | solution.py:93
  56.4 0.2 scatter.19
  56.6 1.2 %fusion.2 = bf16[128,1152]{1,0:T(8,128)(2,1)S(1)} fusion(f32[2,128,1152]{2,1,0:T(8,128)} %convert_add_fusion), kind=kLoop, calls=%fused_computation.16 | loop fusion | bytes 589824 | tf_op jit(solution)/shard_map/convert_element_type | solution.py:96
  57.8 2.8 %collective-permute-start.2 = (bf16[144,1152]{1,0:T(8,128)(2,1)S(1)}, bf16[144,1152]{1,0:T(8,128)(2,1)S(1)}, u32[]{:S(2)}, u32[]{:S(2)}) collective-permute-start(bf16[144,1152]{1,0:T(8,128)(2,1)S(1)} %pad_maximum_fusion.1), channel_id=1, source_target_pairs={{447,0},{384,1},{385,2},{386,3},{387,4},{388,5},{389,6},{390,7},{3... | collective-permute-start | bytes 995336 | tf_op jit(solution)/shard_map/ppermute | solution.py:96
  60.6 30.9 %collective-permute-done.2 = bf16[144,1152]{1,0:T(8,128)(2,1)S(1)} collective-permute-done((bf16[144,1152]{1,0:T(8,128)(2,1)S(1)}, bf16[144,1152]{1,0:T(8,128)(2,1)S(1)}, u32[]{:S(2)}, u32[]{:S(2)}) %collective-permute-start.2) | collective-permute-done | bytes 331808 | tf_op jit(solution)/shard_map/ppermute | solution.py:96
  91.5 0.5 multiply_bitcast_fusion
  92.0 0.9 fusion.1
  92.9 1.0 %convert_reduce_fusion = f32[128,1152]{1,0:T(8,128)} fusion(bf16[4,128,1152]{2,1,0:T(8,128)(2,1)S(1)} %all-to-all-done.1), kind=kLoop, calls=%fused_computation.1 | loop fusion | flops 1032192 | bytes 1769472 | tf_op jit(solution)/shard_map/reduce_sum | solution.py:100
  (28 shorter events, 0.3 us)
Async XLA Ops:
  2.7 9.5 %copy-start.3 = (bf16[128,1152]{1,0:T(8,128)(2,1)S(1)}, bf16[128,1152]{1,0:T(8,128)(2,1)}, u32[]{:S(2)}) copy-start(bf16[128,1152]{1,0:T(8,128)(2,1)} %param.12) | copy-start | bytes 884740
  2.7 35.9 %all-to-all-start = ((bf16[4,128,1152]{2,1,0:T(8,128)(2,1)}), bf16[4,128,1152]{2,1,0:T(8,128)(2,1)S(1)}, u32[]{:S(2)}, u32[]{:S(2)}) async-start(bf16[4,128,1152]{2,1,0:T(8,128)(2,1)} %broadcast_in_dim.20), calls=%async_computation | async-start | bytes 2359296 | tf_op jit(solution)/shard_map/all_to_all | solution.py:70
  12.2 24.1 %collective-permute-start = (bf16[128,1152]{1,0:T(8,128)(2,1)S(1)}, bf16[128,1152]{1,0:T(8,128)(2,1)S(1)}, u32[]{:S(2)}, u32[]{:S(2)}) collective-permute-start(bf16[128,1152]{1,0:T(8,128)(2,1)S(1)} %copy-done.3), channel_id=1, source_target_pairs={{0,447},{1,384},{2,385},{3,386},{4,387},{5,388},{6,389},{7,390},{8... | collective-permute-start | bytes 884744 | tf_op jit(solution)/shard_map/ppermute | solution.py:68
  29.3 9.3 %copy-start.5 = (pred[512]{0:T(512)(128)(4,1)S(1)}, pred[512]{0:T(512)(128)(4,1)}, u32[]{:S(2)}) copy-start(pred[512]{0:T(512)(128)(4,1)} %get-tuple-element.54) | copy-start | bytes 1540
  38.6 2.1 %copy-start.4 = (bf16[512,1152]{1,0:T(8,128)(2,1)}, bf16[512,1152]{1,0:T(8,128)(2,1)S(1)}, u32[]{:S(2)}) copy-start(bf16[512,1152]{1,0:T(8,128)(2,1)S(1)} %constant_dynamic-update-slice_fusion) | copy-start | bytes 3538948
  40.7 0.9 copy-start.1
  41.7 3.2 %copy-start.2 = (bf16[512,512]{1,0:T(8,128)(2,1)S(1)}, bf16[512,512]{1,0:T(8,128)(2,1)}, u32[]{:S(2)}) copy-start(bf16[512,512]{1,0:T(8,128)(2,1)} %copy-done.1) | copy-start | bytes 1572868
  42.9 10.5 %collective-permute-start.1 = (bf16[272,1152]{1,0:T(8,128)(2,1)}, bf16[272,1152]{1,0:T(8,128)(2,1)}, u32[]{:S(2)}, u32[]{:S(2)}) collective-permute-start(bf16[272,1152]{1,0:T(8,128)(2,1)} %pad_maximum_fusion), channel_id=1, source_target_pairs={{0,64},{1,65},{2,66},{3,67},{4,68},{5,69},{6,70},{7,71},{8,72},{9,... | collective-permute-start | bytes 1880072 | tf_op jit(solution)/shard_map/ppermute | solution.py:90
  48.1 44.8 %all-to-all-start.1 = ((bf16[4,128,1152]{2,1,0:T(8,128)(2,1)}), bf16[4,128,1152]{2,1,0:T(8,128)(2,1)S(1)}, u32[]{:S(2)}, u32[]{:S(2)}) async-start(bf16[4,128,1152]{2,1,0:T(8,128)(2,1)} %bitcast.45), calls=%async_computation.1 | async-start | bytes 2359296 | tf_op jit(solution)/shard_map/all_to_all | solution.py:99
  56.4 35.6 %copy-start = (f32[2,128,1152]{2,1,0:T(8,128)S(1)}, f32[2,128,1152]{2,1,0:T(8,128)}, u32[]{:S(2)}) copy-start(f32[2,128,1152]{2,1,0:T(8,128)} %convert_add_fusion) | copy-start | bytes 3538948
  57.8 33.7 %collective-permute-start.2 = (bf16[144,1152]{1,0:T(8,128)(2,1)S(1)}, bf16[144,1152]{1,0:T(8,128)(2,1)S(1)}, u32[]{:S(2)}, u32[]{:S(2)}) collective-permute-start(bf16[144,1152]{1,0:T(8,128)(2,1)S(1)} %pad_maximum_fusion.1), channel_id=1, source_target_pairs={{447,0},{384,1},{385,2},{386,3},{387,4},{388,5},{389,6},{390,7},{3... | collective-permute-start | bytes 995336 | tf_op jit(solution)/shard_map/ppermute | solution.py:96

commit v2 on v1

v2 whole, which is shorter than its diff:
```python
import functools

import jax
import jax.numpy as jnp
import numpy as np
from jax import lax
from jax.experimental import pallas as pl
from jax.experimental.pallas import tpu as pltpu
from jax.sharding import Mesh, PartitionSpec as P

AXES = ("yl", "c", "x", "z", "yh")
BF = jnp.bfloat16
F32 = jnp.float32
EXTRA = 16


def pairs(sizes, fn):
    out = []
    for src in np.ndindex(*sizes):
        out.append((int(np.ravel_multi_index(src, sizes)), int(np.ravel_multi_index(fn(*src), sizes))))
    return out


def visit(sizes):
    nyl, _, nx, nz, _ = sizes

    def fn(yl, c, x, z, yh):
        if yh == 1:
            return nyl - 1 - yl, c, x, z, 0
        k = (x * nz + z - 1) % (nx * nz)
        return nyl - 1 - yl, c, k // nz, k % nz, 1

    return pairs(sizes, fn)


def along_line(sizes, m):
    return pairs(sizes, lambda yl, c, x, z, yh: (yl ^ m, c, x, z, yh))


def contract(left, right, dims):
    return lax.dot_general(left, right, (dims, ((), ())), preferred_element_type=F32)


def slopes_and_loss(positive, factors, images, texts, slopes, loss):
    s, b = factors[0], factors[1]
    z = s * contract(texts[...], images[...], ((1,), (1,))) + b
    pair = positive(z.shape) if positive else None
    u = z if pair is None else jnp.where(pair, -z, z)
    e = jnp.exp(-jnp.abs(u))
    loss[...] = jnp.sum(jnp.maximum(u, 0.0) + jnp.log1p(e), axis=0, keepdims=True)
    slope = s * jnp.where(u >= 0, 1.0, e) / (1.0 + e)
    slopes[...] = (slope if pair is None else jnp.where(pair, -slope, slope)).astype(BF)


def lay(blocks, bundle):
    rows = blocks[0].shape[0]
    for m, block in enumerate(blocks):
        bundle[m * rows : (m + 1) * rows, :] = block[...]


def own_kernel(place, factors, mine, own, far, cross, slopes, loss, bundle):
    lay((own, far, cross), bundle)
    rows = own.shape[0]

    def positive(shape):
        i = lax.broadcasted_iota(jnp.int32, shape, 1) - place[0] * rows
        j = lax.broadcasted_iota(jnp.int32, shape, 0)
        return (i == j) & (j < rows)

    slopes_and_loss(positive, factors, mine, bundle, slopes, loss)


def far_kernel(factors, mine, theirs, own, far, my_slopes, slopes, loss, far_grad, bundle):
    lay((own, far), bundle)
    slopes_and_loss(None, factors, theirs, bundle, slopes, loss)
    rows = own.shape[0]
    far_grad[...] = (
        contract(my_slopes[rows : 2 * rows, :], mine[...], ((1,), (0,)))
        + contract(slopes[rows:, :], theirs[...], ((1,), (0,)))
    ).astype(BF)


def extra_rows(values, width):
    n = values.shape[1]
    hi = values.astype(BF).astype(F32)
    lo = (values - hi).astype(BF).astype(F32)
    row = lax.broadcasted_iota(jnp.int32, (EXTRA, n), 0)
    head = jnp.where(row == 0, hi, jnp.where(row == 1, lo, 0.0))
    return jnp.concatenate([head, jnp.zeros((EXTRA, width - n), F32)], axis=1).astype(BF)


def split_cores(core, total, summed, keep, keep_loss, give):
    rows = keep.shape[0]
    at = pl.multiple_of(core * rows, rows)
    away = pl.multiple_of((1 - core) * rows, rows)
    keep[...] = total[pl.ds(at, rows), :]
    give[:rows, :] = total[pl.ds(away, rows), :].astype(BF)
    zero, one = summed[:, :rows], summed[:, rows:]
    keep_loss[...] = jnp.where(core == 0, zero, one)
    give[rows:, :] = extra_rows(jnp.where(core == 0, one, zero), give.shape[1])


def visit_kernel(
    place, factors, mine, theirs, own, far, near, cross, first_slopes, first_loss, my_loss,
    slopes, near_slopes, loss, keep, keep_loss, give, total, first, second, their_loss,
):
    lay((own, far), first)
    lay((near, cross), second)
    slopes_and_loss(None, factors, theirs, second, slopes, their_loss)
    slopes_and_loss(None, factors, mine, near, near_slopes, loss)
    loss[...] += my_loss[...]
    total[...] = contract(first_slopes[...], first[...], ((0,), (0,))) + contract(
        slopes[...], second[...], ((0,), (0,))
    )
    split_cores(place[0], total, their_loss[...] + first_loss[...], keep, keep_loss, give)


def rest_kernel(
    place, mine, theirs, own, far, near, cross, my_slopes, near_slopes, first_slopes, slopes, loss, after,
    own_grad, near_grad, cross_grad, keep, keep_loss, give, total, bundle,
):
    rows = own.shape[0]

    def text_gradient(of_mine, of_theirs):
        return contract(of_mine, mine[...], ((1,), (0,))) + contract(of_theirs, theirs[...], ((1,), (0,)))

    own_grad[...] = text_gradient(my_slopes[:rows, :], first_slopes[:rows, :])
    near_grad[...] = text_gradient(near_slopes[...], slopes[:rows, :]).astype(BF)
    cross_grad[...] = text_gradient(my_slopes[2 * rows :, :], slopes[rows:, :]).astype(BF)
    lay((own, far, cross), bundle)
    total[...] = contract(my_slopes[...], bundle[...], ((0,), (0,))) + contract(
        near_slopes[...], near[...], ((0,), (0,))
    )
    split_cores(place[0], total, loss[...], keep, keep_loss, give)


def take(place, gathered, rows):
    size = rows + EXTRA
    at = pl.multiple_of((1 - place[0]) * size, size)
    got = gathered[pl.ds(at, rows), :].astype(F32)
    extra = gathered[pl.ds(pl.multiple_of(at + rows, EXTRA), EXTRA), :].astype(F32)
    return got, extra[0:1, :rows] + extra[1:2, :rows]


def visitor_kernel(place, keep, keep_loss, gathered, message):
    rows = keep.shape[0]
    got, got_loss = take(place, gathered, rows)
    message[:rows, :] = (keep[...] + got).astype(BF)
    message[rows:, :] = extra_rows(keep_loss[...] + got_loss, keep.shape[1])


def image_kernel(place, keep, keep_loss, gathered, home, grad, loss):
    rows = keep.shape[0]
    got, got_loss = take(place, gathered, rows)
    grad[...] = keep[...] + got + home[:rows, :].astype(F32)
    extra = home[rows:, :].astype(F32)
    loss[...] = (keep_loss[...] + got_loss + extra[0:1, :rows] + extra[1:2, :rows]) * (1.0 / (16 * rows))


SMEM = pl.BlockSpec(memory_space=pltpu.SMEM)
VMEM = pl.BlockSpec(memory_space=pltpu.VMEM)


def call(kernel, scalars, outs, scratch=()):
    def run(*args):
        return pl.pallas_call(
            kernel,
            out_shape=outs,
            in_specs=[SMEM] * scalars + [VMEM] * (len(args) - scalars),
            out_specs=[VMEM] * len(outs),
            scratch_shapes=list(scratch),
            compiler_params=pltpu.CompilerParams(vmem_limit_bytes=32 * 1024 * 1024),
            cost_estimate=pl.CostEstimate(flops=0, bytes_accessed=0, transcendentals=0),
        )(*args)

    return run


def solution(mesh):
    sizes = (4, 2, 4, 8, 2)
    fine = Mesh(mesh.devices.reshape(sizes), AXES)
    go = visit(sizes)
    back = [(b, a) for a, b in go]
    bar = lax.optimization_barrier
    across = [along_line(sizes, m) for m in range(sizes[0])]

    def shards(images, texts, scale, shift):
        rows, width = images.shape
        shape = jax.ShapeDtypeStruct
        place = lax.axis_index("c").reshape(1).astype(jnp.int32)
        factors = jnp.concatenate([scale, shift])
        block, wide = shape((rows, width), BF), shape((rows, width), F32)
        short, message = shape((1, rows), F32), shape((rows + EXTRA, width), BF)
        line = shape((1, 2 * rows), F32)
        total = pltpu.VMEM((2 * rows, width), F32)

        def slope(blocks):
            return shape((blocks * rows, 2 * rows), BF)

        def bundle(blocks):
            return pltpu.VMEM((blocks * rows, width), BF)

        def both_cores(array):
            return lax.all_gather(array, "c", axis=0, tiled=True)

        far, cross, near = (lax.ppermute(texts, AXES, across[m]) for m in (2, 3, 1))
        visitors = lax.ppermute(images, AXES, go)
        mine = both_cores(images)

        my_slopes, my_loss = call(own_kernel, 2, [slope(3), line], [bundle(3)])(
            place, factors, mine, texts, far, cross
        )
        visitors, my_slopes = bar((visitors, my_slopes))
        theirs = both_cores(visitors)
        slopes0, loss0, far_grad = call(far_kernel, 1, [slope(2), line, block], [bundle(2)])(
            factors, mine, theirs, texts, far, my_slopes
        )
        far_home = lax.ppermute(far_grad, AXES, across[2])
        slopes1, near_slopes, loss, keep_v, keep_loss_v, give_v = call(
            visit_kernel,
            2,
            [slope(2), slope(1), line, wide, short, message],
            [total, bundle(2), bundle(2), pltpu.VMEM((1, 2 * rows), F32)],
        )(place, factors, mine, theirs, texts, far, near, cross, slopes0, loss0, my_loss)
        (sent,) = call(visitor_kernel, 1, [message])(place, keep_v, keep_loss_v, both_cores(give_v))
        home = lax.ppermute(sent, AXES, back)
        own_grad, near_grad, cross_grad, keep, keep_loss, give = call(
            rest_kernel, 1, [wide, block, block, wide, short, message], [total, bundle(3)]
        )(place, mine, theirs, texts, far, near, cross, my_slopes, near_slopes, slopes0, slopes1, loss, sent)
        cross_home = lax.ppermute(cross_grad, AXES, across[3])
        near_home = lax.ppermute(near_grad, AXES, across[1])

        two = own_grad + far_home.astype(F32)
        keep, two = bar((keep, two))
        grad_images, row_loss = call(image_kernel, 1, [wide, short])(
            place, keep, keep_loss, both_cores(give), home
        )
        grad_images, row_loss, two = bar((grad_images, row_loss, two))
        grad_texts = two + (cross_home.astype(F32) + near_home.astype(F32))
        row_loss = row_loss.reshape(rows)
        return grad_images, grad_texts, row_loss

    whole = P(AXES, None)
    return jax.shard_map(
        shards,
        mesh=fine,
        in_specs=(whole, whole, P(), P()),
        out_specs=(whole, whole, P(AXES)),
        check_vma=False,
    )
```

time: 94.4 us -> 83.6 us (0.89)
  waiting for transfers between devices: 37.9 us -> 25.8 us
  Pallas kernels: 0 us -> 7.04 us
  matrix products: 6.1 us -> 0 us
  starting transfers between devices: 32.6 us -> 37.8 us
  local copies, waits for them, and re-layouts: 5.03 us -> 0.01 us
  blocking collectives: 4.44 us -> 9.34 us
  other arithmetic: 5.72 us -> 1.05 us
    ppermute x2 -> x7, starting transfers between devices: 4.82 us -> 26.3 us  [the longest x3 13.9 us: shards(): far, cross, near = (lax.ppermute(texts, AXES, across[m]) for m in (2, 3, 1))]
    all_to_all x2 -> x0, starting transfers between devices: 14.7 us -> none  [the longest x1 9.45 us: shards(): bundle = lax.all_to_all(spread, 'yl', 0, 0).reshape(4 * rows, width)]
    ppermute x2 -> x7, waiting for transfers between devices: 30.9 us -> 21.2 us  [the longest x1 20.9 us: shards(): home = lax.ppermute(sent, AXES, back)]
    pallas_call x0 -> x6, Pallas kernels: none -> 7.04 us  [run(): pl.pallas_call(kernel, out_shape=outs, in_specs=[SMEM] * scalars + [VMEM]...]
    dot_general x3 -> x0, matrix products: 6.1 us -> none  [contract(): lax.dot_general(left, right, (dims, ((), ())), preferred_element_type=F32)]
    all_gather x2 -> x4, blocking collectives: 4.44 us -> 9.34 us  [both_cores(): return lax.all_gather(array, 'c', axis=0, tiled=True)]
    ppermute x1, waiting for transfers between devices: 6.99 us -> 4.56 us  [shards(): visitors = lax.ppermute(images, AXES, go)]
    broadcast_in_dim x1 -> x0, local copies, waits for them, and re-layouts: 2.07 us -> none  [shards(): spread = jnp.broadcast_to(texts[None], (4, rows, width))]
  transfers between devices with their start and end apart: 5 -> 8, of which waited for: 2 -> 3; matrix products, arithmetic and copies ran while one was open for 10% -> 0% of each run, Pallas kernels for 0% -> 8%
where the time goes in v2:
time: 83.6 us; the launch traced here: 83.1 us
  starting transfers between devices  37.8 us (45%)
  waiting for transfers between devices  25.8 us (31%)
  blocking collectives  9.34 us (11%)
  Pallas kernels  7.04 us (8%)
  between operations  2.02 us (2%)
  other arithmetic  1.05 us (1%)
    ppermute x1, waiting for transfers between devices, shards(): home = lax.ppermute(sent, AXES, back)  20.9 us
    ppermute x3, starting transfers between devices, shards(): far, cross, near = (lax.ppermute(texts, AXES, across[m]) for m in (2, 3, 1))  13.9 us
    ppermute x1, starting transfers between devices, shards(): visitors = lax.ppermute(images, AXES, go)  11.6 us
    all_gather x4, blocking collectives, both_cores(): return lax.all_gather(array, 'c', axis=0, tiled=True)  9.34 us
    pallas_call x6, Pallas kernels, run(): pl.pallas_call(kernel, out_shape=outs, in_specs=[SMEM] * scalars + [VMEM]...  7.04 us
    ppermute x1, waiting for transfers between devices, shards(): visitors = lax.ppermute(images, AXES, go)  4.56 us
    ppermute x1, starting transfers between devices, shards(): home = lax.ppermute(sent, AXES, back)  3.95 us
    ppermute x1, starting transfers between devices, shards(): near_home = lax.ppermute(near_grad, AXES, across[1])  3.93 us
  transfers between devices with their start and end apart: 8, of which 3 were waited for; matrix products, arithmetic and copies ran while one was open for 0% of the time, Pallas kernels for 8%

profile of v2, /device:TPU:8, one launch (start us, length us, event | category | flops | bytes accessed | tf_op | source)
XLA Modules:
  0.0 83.1 jit_solution(16451241419503829610)
XLA Ops:
  0.6 3.5 %collective-permute-start.2 = (bf16[128,1152]{1,0:T(8,128)(2,1)}, bf16[128,1152]{1,0:T(8,128)(2,1)S(1)}, u32[]{:S(2)}, u32[]{:S(2)}) collective-permute-start(bf16[128,1152]{1,0:T(8,128)(2,1)} %own.7), channel_id=1, source_target_pairs={{0,384},{1,385},{2,386},{3,387},{4,388},{5,389},{6,390},{7,391},{8... | collective-permute-start | bytes 884744 | tf_op jit(solution)/shard_map/ppermute | solution.py:206
  4.1 8.5 %collective-permute-start.1 = (bf16[128,1152]{1,0:T(8,128)(2,1)}, bf16[128,1152]{1,0:T(8,128)(2,1)S(1)}, u32[]{:S(2)}, u32[]{:S(2)}) collective-permute-start(bf16[128,1152]{1,0:T(8,128)(2,1)} %own.7), channel_id=1, source_target_pairs={{0,256},{1,257},{2,258},{3,259},{4,260},{5,261},{6,262},{7,263},{8... | collective-permute-start | bytes 884744 | tf_op jit(solution)/shard_map/ppermute | solution.py:206
  12.7 11.6 %collective-permute-start = (bf16[128,1152]{1,0:T(8,128)(2,1)}, bf16[128,1152]{1,0:T(8,128)(2,1)S(1)}, u32[]{:S(2)}, u32[]{:S(2)}) collective-permute-start(bf16[128,1152]{1,0:T(8,128)(2,1)} %param.4), channel_id=1, source_target_pairs={{0,447},{1,384},{2,385},{3,386},{4,387},{5,388},{6,389},{7,390},{8... | collective-permute-start | bytes 884744 | tf_op jit(solution)/shard_map/ppermute | solution.py:207
  24.2 1.9 %collective-permute-start.3 = (bf16[128,1152]{1,0:T(8,128)(2,1)}, bf16[128,1152]{1,0:T(8,128)(2,1)S(1)}, u32[]{:S(2)}, u32[]{:S(2)}) collective-permute-start(bf16[128,1152]{1,0:T(8,128)(2,1)} %own.7), channel_id=1, source_target_pairs={{0,128},{1,129},{2,130},{3,131},{4,132},{5,133},{6,134},{7,135},{8... | collective-permute-start | bytes 884744 | tf_op jit(solution)/shard_map/ppermute | solution.py:206
  27.5 0.1 pad_maximum_fusion.factors
  27.5 2.6 %all_gather.12.mine = bf16[256,1152]{1,0:T(8,128)(2,1)S(1)} all-gather(bf16[128,1152]{1,0:T(8,128)(2,1)} %param.4), channel_id=1, replica_groups=mesh['yl'=4,'c'=2,'x'=4,'z'=8,'yh'=2] {'c'}, dimensions={0}, use_global_device_ids=true | all-gather | bytes 884736 | tf_op jit(solution)/shard_map/all_gather | solution.py:204
  30.1 1.3 %shard_map.67 = (bf16[384,256]{1,0:T(8,128)(2,1)S(1)}, f32[1,256]{1,0:T(1,128)S(1)}) custom-call(s32[1]{0:T(128)} %bitcast.place, f32[2]{0:T(128)S(1)} %pad_maximum_fusion.factors, bf16[256,1152]{1,0:T(8,128)(2,1)S(1)} %all_gather.12.mine, bf16[128,1152]{1,0:T(8,128)(2,1)S(1)} %copy-done, bf16[128,1152]{1,0:T(8,128)(2,1)S(1)} %collective-permute-done.1.far, ...), custom_call_target="tpu_custom_call" | custom-call | tf_op jit(solution)/shard_map/pallas_call | solution.py:166
  31.4 4.6 %collective-permute-done = bf16[128,1152]{1,0:T(8,128)(2,1)S(1)} collective-permute-done((bf16[128,1152]{1,0:T(8,128)(2,1)}, bf16[128,1152]{1,0:T(8,128)(2,1)S(1)}, u32[]{:S(2)}, u32[]{:S(2)}) %collective-permute-start) | collective-permute-done | bytes 294944 | tf_op jit(solution)/shard_map/ppermute | solution.py:207
  35.9 2.2 %all_gather.13.theirs = bf16[256,1152]{1,0:T(8,128)(2,1)S(1)} all-gather(bf16[128,1152]{1,0:T(8,128)(2,1)S(1)} %collective-permute-done), channel_id=1, replica_groups=mesh['yl'=4,'c'=2,'x'=4,'z'=8,'yh'=2] {'c'}, dimensions={0}, use_global_device_ids=true | all-gather | bytes 884736 | tf_op jit(solution)/shard_map/all_gather | solution.py:204
  38.2 1.6 %shard_map.68 = (bf16[256,256]{1,0:T(8,128)(2,1)S(1)}, f32[1,256]{1,0:T(1,128)S(1)}, bf16[128,1152]{1,0:T(8,128)(2,1)S(1)}) custom-call(f32[2]{0:T(128)S(1)} %pad_maximum_fusion.factors, bf16[256,1152]{1,0:T(8,128)(2,1)S(1)} %all_gather.12.mine, bf16[256,1152]{1,0:T(8,128)(2,1)S(1)} %all_gather.13.theirs, bf16[128,1152]{1,0:T(8,128)(2,1)S(1)} %copy-done, ...), custom_call_target="tpu_custom_call" | custom-call | tf_op jit(solution)/shard_map/pallas_call | solution.py:166
  39.8 1.9 %collective-permute-start.4 = (bf16[128,1152]{1,0:T(8,128)(2,1)S(1)}, bf16[128,1152]{1,0:T(8,128)(2,1)S(1)}, u32[]{:S(2)}, u32[]{:S(2)}) collective-permute-start(bf16[128,1152]{1,0:T(8,128)(2,1)S(1)} %get-tuple-element.43), channel_id=1, source_target_pairs={{0,256},{1,257},{2,258},{3,259},{4,260},{5,261},{6,262},{7,263},{8... | collective-permute-start | bytes 884744 | tf_op jit(solution)/shard_map/ppermute | solution.py:218
  41.7 0.3 collective-permute-done.3.near
  42.0 1.8 %shard_map.69 = (bf16[256,256]{1,0:T(8,128)(2,1)S(1)}, bf16[128,256]{1,0:T(8,128)(2,1)S(1)}, f32[1,256]{1,0:T(1,128)S(1)}, f32[128,1152]{1,0:T(8,128)S(1)}, f32[...) custom-call(s32[1]{0:T(128)} %bitcast.place, f32[2]{0:T(128)S(1)} %pad_maximum_fusion.factors, ...), custom_call_target="tpu_custom_call" | custom-call | tf_op jit(solution)/shard_map/pallas_call | solution.py:166
  43.9 2.3 %all_gather.14.gathered = bf16[288,1152]{1,0:T(8,128)(2,1)S(1)} all-gather(bf16[144,1152]{1,0:T(8,128)(2,1)S(1)} %get-tuple-element.40), channel_id=1, replica_groups=mesh['yl'=4,'c'=2,'x'=4,'z'=8,'yh'=2] {'c'}, dimensions={0}, use_global_device_ids=true | all-gather | bytes 995328 | tf_op jit(solution)/shard_map/all_gather | solution.py:204
  46.2 0.1 shard_map.70.after
  46.3 4.0 %collective-permute-start.5 = (bf16[144,1152]{1,0:T(8,128)(2,1)S(1)}, bf16[144,1152]{1,0:T(8,128)(2,1)S(1)}, u32[]{:S(2)}, u32[]{:S(2)}) collective-permute-start(bf16[144,1152]{1,0:T(8,128)(2,1)S(1)} %shard_map.70.after), channel_id=1, source_target_pairs={{447,0},{384,1},{385,2},{386,3},{387,4},{388,5},{389,6},{390,7},{3... | collective-permute-start | bytes 995336 | tf_op jit(solution)/shard_map/ppermute | solution.py:226
  50.2 1.3 %shard_map.71 = (f32[128,1152]{1,0:T(8,128)S(1)}, bf16[128,1152]{1,0:T(8,128)(2,1)S(1)}, bf16[128,1152]{1,0:T(8,128)(2,1)S(1)}, f32[128,1152]{1,0:T(8,128)S(1)},...) custom-call(s32[1]{0:T(128)} %bitcast.place, bf16[256,1152]{1,0:T(8,128)(2,1)S(1)} %all_gather.12.mine, ...), custom_call_target="tpu_custom_call" | custom-call | tf_op jit(solution)/shard_map/pallas_call | solution.py:166
  51.5 2.5 %collective-permute-start.6 = (bf16[128,1152]{1,0:T(8,128)(2,1)S(1)}, bf16[128,1152]{1,0:T(8,128)(2,1)S(1)}, u32[]{:S(2)}, u32[]{:S(2)}) collective-permute-start(bf16[128,1152]{1,0:T(8,128)(2,1)S(1)} %get-tuple-element.52), channel_id=1, source_target_pairs={{0,384},{1,385},{2,386},{3,387},{4,388},{5,389},{6,390},{7,391},{8... | collective-permute-start | bytes 884744 | tf_op jit(solution)/shard_map/ppermute | solution.py:230
  54.0 3.9 %collective-permute-start.7 = (bf16[128,1152]{1,0:T(8,128)(2,1)S(1)}, bf16[128,1152]{1,0:T(8,128)(2,1)S(1)}, u32[]{:S(2)}, u32[]{:S(2)}) collective-permute-start(bf16[128,1152]{1,0:T(8,128)(2,1)S(1)} %get-tuple-element.53), channel_id=1, source_target_pairs={{0,128},{1,129},{2,130},{3,131},{4,132},{5,133},{6,134},{7,135},{8... | collective-permute-start | bytes 884744 | tf_op jit(solution)/shard_map/ppermute | solution.py:231
  58.0 2.3 %all_gather.15.gathered = bf16[288,1152]{1,0:T(8,128)(2,1)S(1)} all-gather(bf16[144,1152]{1,0:T(8,128)(2,1)S(1)} %get-tuple-element.46), channel_id=1, replica_groups=mesh['yl'=4,'c'=2,'x'=4,'z'=8,'yh'=2] {'c'}, dimensions={0}, use_global_device_ids=true | all-gather | bytes 995328 | tf_op jit(solution)/shard_map/all_gather | solution.py:204
  60.3 0.1 convert_add_fusion
  60.3 20.9 %collective-permute-done.5.home = bf16[144,1152]{1,0:T(8,128)(2,1)S(1)} collective-permute-done((bf16[144,1152]{1,0:T(8,128)(2,1)S(1)}, bf16[144,1152]{1,0:T(8,128)(2,1)S(1)}, u32[]{:S(2)}, u32[]{:S(2)}) %collective-permute-start.5) | collective-permute-done | bytes 331808 | tf_op jit(solution)/shard_map/ppermute | solution.py:226
  81.2 0.9 %shard_map.72 = (f32[128,1152]{1,0:T(8,128)}, f32[1,128]{1,0:T(1,128)}) custom-call(s32[1]{0:T(128)} %bitcast.place, f32[128,1152]{1,0:T(8,128)S(1)} %get-tuple-element.44.keep, f32[1,128]{1,0:T(1,128)S(1)} %get-tuple-element.45.keep_loss, bf16[288,1152]{1,0:T(8,128)(2,1)S(1)} %all_gather.15.gathered, bf16[144,1152]{1,0:T(8,128)(2,1)S(1)} %collective-permute-done.5.home), custom_call_target="tpu_custom_call" | custom-call | tf_op jit(solution)/shard_map/pallas_call | solution.py:166
  82.1 0.9 %add_add_fusion = f32[128,1152]{1,0:T(8,128)} fusion(f32[128,1152]{1,0:T(8,128)S(1)} %convert_add_fusion, bf16[128,1152]{1,0:T(8,128)(2,1)S(1)} %collective-permute-done.7, bf16[128,1152]{1,0:T(8,128)(2,1)S(1)} %collective-permute-done.6), kind=kLoop, calls=%fused_computation | loop fusion | flops 589824 | bytes 1769472 | tf_op jit(solution)/shard_map/add | solution.py:239
  (7 shorter events, 0.0 us)
Async XLA Ops:
  0.6 29.5 %collective-permute-start.2 = (bf16[128,1152]{1,0:T(8,128)(2,1)}, bf16[128,1152]{1,0:T(8,128)(2,1)S(1)}, u32[]{:S(2)}, u32[]{:S(2)}) collective-permute-start(bf16[128,1152]{1,0:T(8,128)(2,1)} %own.7), channel_id=1, source_target_pairs={{0,384},{1,385},{2,386},{3,387},{4,388},{5,389},{6,390},{7,391},{8... | collective-permute-start | bytes 884744 | tf_op jit(solution)/shard_map/ppermute | solution.py:206
  4.1 26.0 %collective-permute-start.1 = (bf16[128,1152]{1,0:T(8,128)(2,1)}, bf16[128,1152]{1,0:T(8,128)(2,1)S(1)}, u32[]{:S(2)}, u32[]{:S(2)}) collective-permute-start(bf16[128,1152]{1,0:T(8,128)(2,1)} %own.7), channel_id=1, source_target_pairs={{0,256},{1,257},{2,258},{3,259},{4,260},{5,261},{6,262},{7,263},{8... | collective-permute-start | bytes 884744 | tf_op jit(solution)/shard_map/ppermute | solution.py:206
  12.7 23.3 %collective-permute-start = (bf16[128,1152]{1,0:T(8,128)(2,1)}, bf16[128,1152]{1,0:T(8,128)(2,1)S(1)}, u32[]{:S(2)}, u32[]{:S(2)}) collective-permute-start(bf16[128,1152]{1,0:T(8,128)(2,1)} %param.4), channel_id=1, source_target_pairs={{0,447},{1,384},{2,385},{3,386},{4,387},{5,388},{6,389},{7,390},{8... | collective-permute-start | bytes 884744 | tf_op jit(solution)/shard_map/ppermute | solution.py:207
  24.2 17.8 %collective-permute-start.3 = (bf16[128,1152]{1,0:T(8,128)(2,1)}, bf16[128,1152]{1,0:T(8,128)(2,1)S(1)}, u32[]{:S(2)}, u32[]{:S(2)}) collective-permute-start(bf16[128,1152]{1,0:T(8,128)(2,1)} %own.7), channel_id=1, source_target_pairs={{0,128},{1,129},{2,130},{3,131},{4,132},{5,133},{6,134},{7,135},{8... | collective-permute-start | bytes 884744 | tf_op jit(solution)/shard_map/ppermute | solution.py:206
  27.5 2.6 %copy-start = (bf16[128,1152]{1,0:T(8,128)(2,1)S(1)}, bf16[128,1152]{1,0:T(8,128)(2,1)}, u32[]{:S(2)}) copy-start(bf16[128,1152]{1,0:T(8,128)(2,1)} %own.7) | copy-start | bytes 884740
  39.8 20.5 %collective-permute-start.4 = (bf16[128,1152]{1,0:T(8,128)(2,1)S(1)}, bf16[128,1152]{1,0:T(8,128)(2,1)S(1)}, u32[]{:S(2)}, u32[]{:S(2)}) collective-permute-start(bf16[128,1152]{1,0:T(8,128)(2,1)S(1)} %get-tuple-element.43), channel_id=1, source_target_pairs={{0,256},{1,257},{2,258},{3,259},{4,260},{5,261},{6,262},{7,263},{8... | collective-permute-start | bytes 884744 | tf_op jit(solution)/shard_map/ppermute | solution.py:218
  46.3 35.0 %collective-permute-start.5 = (bf16[144,1152]{1,0:T(8,128)(2,1)S(1)}, bf16[144,1152]{1,0:T(8,128)(2,1)S(1)}, u32[]{:S(2)}, u32[]{:S(2)}) collective-permute-start(bf16[144,1152]{1,0:T(8,128)(2,1)S(1)} %shard_map.70.after), channel_id=1, source_target_pairs={{447,0},{384,1},{385,2},{386,3},{387,4},{388,5},{389,6},{390,7},{3... | collective-permute-start | bytes 995336 | tf_op jit(solution)/shard_map/ppermute | solution.py:226
  51.5 30.6 %collective-permute-start.6 = (bf16[128,1152]{1,0:T(8,128)(2,1)S(1)}, bf16[128,1152]{1,0:T(8,128)(2,1)S(1)}, u32[]{:S(2)}, u32[]{:S(2)}) collective-permute-start(bf16[128,1152]{1,0:T(8,128)(2,1)S(1)} %get-tuple-element.52), channel_id=1, source_target_pairs={{0,384},{1,385},{2,386},{3,387},{4,388},{5,389},{6,390},{7,391},{8... | collective-permute-start | bytes 884744 | tf_op jit(solution)/shard_map/ppermute | solution.py:230
  54.0 28.1 %collective-permute-start.7 = (bf16[128,1152]{1,0:T(8,128)(2,1)S(1)}, bf16[128,1152]{1,0:T(8,128)(2,1)S(1)}, u32[]{:S(2)}, u32[]{:S(2)}) collective-permute-start(bf16[128,1152]{1,0:T(8,128)(2,1)S(1)} %get-tuple-element.53), channel_id=1, source_target_pairs={{0,128},{1,129},{2,130},{3,131},{4,132},{5,133},{6,134},{7,135},{8... | collective-permute-start | bytes 884744 | tf_op jit(solution)/shard_map/ppermute | solution.py:231

commit v3 on v2

--- a/solution.py
+++ b/solution.py
@@ -58,8 +58,8 @@
         bundle[m * rows : (m + 1) * rows, :] = block[...]
 
 
-def own_kernel(place, factors, mine, own, far, cross, slopes, loss, bundle):
-    lay((own, far, cross), bundle)
+def own_kernel(place, factors, mine, own, cross, near, slopes, loss, bundle):
+    lay((own, cross, near), bundle)
     rows = own.shape[0]
 
     def positive(shape):
@@ -70,11 +70,11 @@
     slopes_and_loss(positive, factors, mine, bundle, slopes, loss)
 
 
-def far_kernel(factors, mine, theirs, own, far, my_slopes, slopes, loss, far_grad, bundle):
-    lay((own, far), bundle)
+def cross_kernel(factors, mine, theirs, own, cross, my_slopes, slopes, loss, cross_grad, bundle):
+    lay((own, cross), bundle)
     slopes_and_loss(None, factors, theirs, bundle, slopes, loss)
     rows = own.shape[0]
-    far_grad[...] = (
+    cross_grad[...] = (
         contract(my_slopes[rows : 2 * rows, :], mine[...], ((1,), (0,)))
         + contract(slopes[rows:, :], theirs[...], ((1,), (0,)))
     ).astype(BF)
@@ -101,13 +101,13 @@
 
 
 def visit_kernel(
-    place, factors, mine, theirs, own, far, near, cross, first_slopes, first_loss, my_loss,
-    slopes, near_slopes, loss, keep, keep_loss, give, total, first, second, their_loss,
+    place, factors, mine, theirs, own, cross, far, near, first_slopes, first_loss, my_loss,
+    slopes, far_slopes, loss, keep, keep_loss, give, total, first, second, their_loss,
 ):
-    lay((own, far), first)
-    lay((near, cross), second)
+    lay((own, cross), first)
+    lay((far, near), second)
     slopes_and_loss(None, factors, theirs, second, slopes, their_loss)
-    slopes_and_loss(None, factors, mine, near, near_slopes, loss)
+    slopes_and_loss(None, factors, mine, far, far_slopes, loss)
     loss[...] += my_loss[...]
     total[...] = contract(first_slopes[...], first[...], ((0,), (0,))) + contract(
         slopes[...], second[...], ((0,), (0,))
@@ -116,8 +116,8 @@
 
 
 def rest_kernel(
-    place, mine, theirs, own, far, near, cross, my_slopes, near_slopes, first_slopes, slopes, loss, after,
-    own_grad, near_grad, cross_grad, keep, keep_loss, give, total, bundle,
+    place, mine, theirs, own, cross, far, near, my_slopes, far_slopes, first_slopes, slopes, loss, after,
+    own_grad, far_grad, near_grad, keep, keep_loss, give, total, bundle,
 ):
     rows = own.shape[0]
 
@@ -125,11 +125,11 @@
         return contract(of_mine, mine[...], ((1,), (0,))) + contract(of_theirs, theirs[...], ((1,), (0,)))
 
     own_grad[...] = text_gradient(my_slopes[:rows, :], first_slopes[:rows, :])
-    near_grad[...] = text_gradient(near_slopes[...], slopes[:rows, :]).astype(BF)
-    cross_grad[...] = text_gradient(my_slopes[2 * rows :, :], slopes[rows:, :]).astype(BF)
-    lay((own, far, cross), bundle)
+    far_grad[...] = text_gradient(far_slopes[...], slopes[:rows, :]).astype(BF)
+    near_grad[...] = text_gradient(my_slopes[2 * rows :, :], slopes[rows:, :]).astype(BF)
+    lay((own, cross, near), bundle)
     total[...] = contract(my_slopes[...], bundle[...], ((0,), (0,))) + contract(
-        near_slopes[...], near[...], ((0,), (0,))
+        far_slopes[...], far[...], ((0,), (0,))
     )
     split_cores(place[0], total, loss[...], keep, keep_loss, give)
 
@@ -203,40 +203,40 @@
         def both_cores(array):
             return lax.all_gather(array, "c", axis=0, tiled=True)
 
-        far, cross, near = (lax.ppermute(texts, AXES, across[m]) for m in (2, 3, 1))
+        cross, near, far = (lax.ppermute(texts, AXES, across[m]) for m in (3, 1, 2))
         visitors = lax.ppermute(images, AXES, go)
         mine = both_cores(images)
 
         my_slopes, my_loss = call(own_kernel, 2, [slope(3), line], [bundle(3)])(
-            place, factors, mine, texts, far, cross
+            place, factors, mine, texts, cross, near
         )
         visitors, my_slopes = bar((visitors, my_slopes))
         theirs = both_cores(visitors)
-        slopes0, loss0, far_grad = call(far_kernel, 1, [slope(2), line, block], [bundle(2)])(
-            factors, mine, theirs, texts, far, my_slopes
+        slopes0, loss0, cross_grad = call(cross_kernel, 1, [slope(2), line, block], [bundle(2)])(
+            factors, mine, theirs, texts, cross, my_slopes
         )
-        far_home = lax.ppermute(far_grad, AXES, across[2])
-        slopes1, near_slopes, loss, keep_v, keep_loss_v, give_v = call(
+        cross_home = lax.ppermute(cross_grad, AXES, across[3])
+        slopes1, far_slopes, loss, keep_v, keep_loss_v, give_v = call(
             visit_kernel,
             2,
             [slope(2), slope(1), line, wide, short, message],
             [total, bundle(2), bundle(2), pltpu.VMEM((1, 2 * rows), F32)],
-        )(place, factors, mine, theirs, texts, far, near, cross, slopes0, loss0, my_loss)
+        )(place, factors, mine, theirs, texts, cross, far, near, slopes0, loss0, my_loss)
         (sent,) = call(visitor_kernel, 1, [message])(place, keep_v, keep_loss_v, both_cores(give_v))
         home = lax.ppermute(sent, AXES, back)
-        own_grad, near_grad, cross_grad, keep, keep_loss, give = call(
+        own_grad, far_grad, near_grad, keep, keep_loss, give = call(
             rest_kernel, 1, [wide, block, block, wide, short, message], [total, bundle(3)]
-        )(place, mine, theirs, texts, far, near, cross, my_slopes, near_slopes, slopes0, slopes1, loss, sent)
-        cross_home = lax.ppermute(cross_grad, AXES, across[3])
+        )(place, mine, theirs, texts, cross, far, near, my_slopes, far_slopes, slopes0, slopes1, loss, sent)
+        far_home = lax.ppermute(far_grad, AXES, across[2])
         near_home = lax.ppermute(near_grad, AXES, across[1])
 
-        two = own_grad + far_home.astype(F32)
+        two = own_grad + cross_home.astype(F32)
         keep, two = bar((keep, two))
         grad_images, row_loss = call(image_kernel, 1, [wide, short])(
             place, keep, keep_loss, both_cores(give), home
         )
         grad_images, row_loss, two = bar((grad_images, row_loss, two))
-        grad_texts = two + (cross_home.astype(F32) + near_home.astype(F32))
+        grad_texts = two + (far_home.astype(F32) + near_home.astype(F32))
         row_loss = row_loss.reshape(rows)
         return grad_images, grad_texts, row_loss
 

time: 83.6 us -> 75.7 us (0.906)
  the two profiles are of different devices: /device:TPU:8 before, /device:TPU:1 now
where the time goes in v3:
time: 75.7 us; the launch traced here: 75.3 us
  starting transfers between devices  38.3 us (51%)
  waiting for transfers between devices  14.3 us (19%)
  blocking collectives  12.6 us (17%)
  Pallas kernels  7.04 us (9%)
  between operations  2.03 us (3%)
  other arithmetic  1.05 us (1%)
    ppermute x1, starting transfers between devices, shards(): visitors = lax.ppermute(images, AXES, go)  15.3 us
    all_gather x4, blocking collectives, both_cores(): return lax.all_gather(array, 'c', axis=0, tiled=True)  12.6 us
    ppermute x3, starting transfers between devices, shards(): cross, near, far = (lax.ppermute(texts, AXES, across[m]) for m in (3, 1, 2))  10.8 us
    ppermute x1, waiting for transfers between devices, shards(): home = lax.ppermute(sent, AXES, back)  10.8 us
    pallas_call x6, Pallas kernels, run(): pl.pallas_call(kernel, out_shape=outs, in_specs=[SMEM] * scalars + [VMEM]...  7.04 us
    ppermute x1, starting transfers between devices, shards(): near_home = lax.ppermute(near_grad, AXES, across[1])  5.13 us
    ppermute x1, waiting for transfers between devices, shards(): visitors = lax.ppermute(images, AXES, go)  3.41 us
    ppermute x1, starting transfers between devices, shards(): cross_home = lax.ppermute(cross_grad, AXES, across[3])  3.2 us
  transfers between devices with their start and end apart: 8, of which 2 were waited for; matrix products, arithmetic and copies ran while one was open for 0% of the time, Pallas kernels for 9%

profile of v3, /device:TPU:1, one launch (start us, length us, event | category | flops | bytes accessed | tf_op | source)
XLA Modules:
  0.0 75.3 jit_solution(10694527273639256777)
XLA Ops:
  0.6 4.0 %collective-permute-start.2 = (bf16[128,1152]{1,0:T(8,128)(2,1)}, bf16[128,1152]{1,0:T(8,128)(2,1)S(1)}, u32[]{:S(2)}, u32[]{:S(2)}) collective-permute-start(bf16[128,1152]{1,0:T(8,128)(2,1)} %own.7), channel_id=1, source_target_pairs={{0,128},{1,129},{2,130},{3,131},{4,132},{5,133},{6,134},{7,135},{8... | collective-permute-start | bytes 884744 | tf_op jit(solution)/shard_map/ppermute | solution.py:206
  4.7 4.1 %collective-permute-start.1 = (bf16[128,1152]{1,0:T(8,128)(2,1)}, bf16[128,1152]{1,0:T(8,128)(2,1)S(1)}, u32[]{:S(2)}, u32[]{:S(2)}) collective-permute-start(bf16[128,1152]{1,0:T(8,128)(2,1)} %own.7), channel_id=1, source_target_pairs={{0,384},{1,385},{2,386},{3,387},{4,388},{5,389},{6,390},{7,391},{8... | collective-permute-start | bytes 884744 | tf_op jit(solution)/shard_map/ppermute | solution.py:206
  8.8 15.3 %collective-permute-start = (bf16[128,1152]{1,0:T(8,128)(2,1)}, bf16[128,1152]{1,0:T(8,128)(2,1)S(1)}, u32[]{:S(2)}, u32[]{:S(2)}) collective-permute-start(bf16[128,1152]{1,0:T(8,128)(2,1)} %param.4), channel_id=1, source_target_pairs={{0,447},{1,384},{2,385},{3,386},{4,387},{5,388},{6,389},{7,390},{8... | collective-permute-start | bytes 884744 | tf_op jit(solution)/shard_map/ppermute | solution.py:207
  24.1 2.7 %collective-permute-start.3 = (bf16[128,1152]{1,0:T(8,128)(2,1)}, bf16[128,1152]{1,0:T(8,128)(2,1)S(1)}, u32[]{:S(2)}, u32[]{:S(2)}) collective-permute-start(bf16[128,1152]{1,0:T(8,128)(2,1)} %own.7), channel_id=1, source_target_pairs={{0,256},{1,257},{2,258},{3,259},{4,260},{5,261},{6,262},{7,263},{8... | collective-permute-start | bytes 884744 | tf_op jit(solution)/shard_map/ppermute | solution.py:206
  28.1 0.1 pad_maximum_fusion.factors
  28.2 3.7 %all_gather.12.mine = bf16[256,1152]{1,0:T(8,128)(2,1)S(1)} all-gather(bf16[128,1152]{1,0:T(8,128)(2,1)} %param.4), channel_id=1, replica_groups=mesh['yl'=4,'c'=2,'x'=4,'z'=8,'yh'=2] {'c'}, dimensions={0}, use_global_device_ids=true | all-gather | bytes 884736 | tf_op jit(solution)/shard_map/all_gather | solution.py:204
  31.9 0.0 collective-permute-done.2.near
  31.9 1.3 %shard_map.67 = (bf16[384,256]{1,0:T(8,128)(2,1)S(1)}, f32[1,256]{1,0:T(1,128)S(1)}) custom-call(s32[1]{0:T(128)} %bitcast.place, f32[2]{0:T(128)S(1)} %pad_maximum_fusion.factors, bf16[256,1152]{1,0:T(8,128)(2,1)S(1)} %all_gather.12.mine, bf16[128,1152]{1,0:T(8,128)(2,1)S(1)} %copy-done, bf16[128,1152]{1,0:T(8,128)(2,1)S(1)} %collective-permute-done.1.cross, ...), custom_call_target="tpu_custom_call" | custom-call | tf_op jit(solution)/shard_map/pallas_call | solution.py:166
  33.2 3.4 %collective-permute-done = bf16[128,1152]{1,0:T(8,128)(2,1)S(1)} collective-permute-done((bf16[128,1152]{1,0:T(8,128)(2,1)}, bf16[128,1152]{1,0:T(8,128)(2,1)S(1)}, u32[]{:S(2)}, u32[]{:S(2)}) %collective-permute-start) | collective-permute-done | bytes 294944 | tf_op jit(solution)/shard_map/ppermute | solution.py:207
  36.6 3.2 %all_gather.13.theirs = bf16[256,1152]{1,0:T(8,128)(2,1)S(1)} all-gather(bf16[128,1152]{1,0:T(8,128)(2,1)S(1)} %collective-permute-done), channel_id=1, replica_groups=mesh['yl'=4,'c'=2,'x'=4,'z'=8,'yh'=2] {'c'}, dimensions={0}, use_global_device_ids=true | all-gather | bytes 884736 | tf_op jit(solution)/shard_map/all_gather | solution.py:204
  39.8 1.6 %shard_map.68 = (bf16[256,256]{1,0:T(8,128)(2,1)S(1)}, f32[1,256]{1,0:T(1,128)S(1)}, bf16[128,1152]{1,0:T(8,128)(2,1)S(1)}) custom-call(f32[2]{0:T(128)S(1)} %pad_maximum_fusion.factors, bf16[256,1152]{1,0:T(8,128)(2,1)S(1)} %all_gather.12.mine, bf16[256,1152]{1,0:T(8,128)(2,1)S(1)} %all_gather.13.theirs, bf16[128,1152]{1,0:T(8,128)(2,1)S(1)} %copy-done, ...), custom_call_target="tpu_custom_call" | custom-call | tf_op jit(solution)/shard_map/pallas_call | solution.py:166
  41.4 3.2 %collective-permute-start.4 = (bf16[128,1152]{1,0:T(8,128)(2,1)S(1)}, bf16[128,1152]{1,0:T(8,128)(2,1)S(1)}, u32[]{:S(2)}, u32[]{:S(2)}) collective-permute-start(bf16[128,1152]{1,0:T(8,128)(2,1)S(1)} %get-tuple-element.43), channel_id=1, source_target_pairs={{0,384},{1,385},{2,386},{3,387},{4,388},{5,389},{6,390},{7,391},{8... | collective-permute-start | bytes 884744 | tf_op jit(solution)/shard_map/ppermute | solution.py:218
  44.7 1.9 %shard_map.69 = (bf16[256,256]{1,0:T(8,128)(2,1)S(1)}, bf16[128,256]{1,0:T(8,128)(2,1)S(1)}, f32[1,256]{1,0:T(1,128)S(1)}, f32[128,1152]{1,0:T(8,128)S(1)}, f32[...) custom-call(s32[1]{0:T(128)} %bitcast.place, f32[2]{0:T(128)S(1)} %pad_maximum_fusion.factors, ...), custom_call_target="tpu_custom_call" | custom-call | tf_op jit(solution)/shard_map/pallas_call | solution.py:166
  46.5 2.6 %all_gather.14.gathered = bf16[288,1152]{1,0:T(8,128)(2,1)S(1)} all-gather(bf16[144,1152]{1,0:T(8,128)(2,1)S(1)} %get-tuple-element.40), channel_id=1, replica_groups=mesh['yl'=4,'c'=2,'x'=4,'z'=8,'yh'=2] {'c'}, dimensions={0}, use_global_device_ids=true | all-gather | bytes 995328 | tf_op jit(solution)/shard_map/all_gather | solution.py:204
  49.1 0.1 shard_map.70.after
  49.2 1.9 %collective-permute-start.5 = (bf16[144,1152]{1,0:T(8,128)(2,1)S(1)}, bf16[144,1152]{1,0:T(8,128)(2,1)S(1)}, u32[]{:S(2)}, u32[]{:S(2)}) collective-permute-start(bf16[144,1152]{1,0:T(8,128)(2,1)S(1)} %shard_map.70.after), channel_id=1, source_target_pairs={{447,0},{384,1},{385,2},{386,3},{387,4},{388,5},{389,6},{390,7},{3... | collective-permute-start | bytes 995336 | tf_op jit(solution)/shard_map/ppermute | solution.py:226
  51.1 1.3 %shard_map.71 = (f32[128,1152]{1,0:T(8,128)S(1)}, bf16[128,1152]{1,0:T(8,128)(2,1)S(1)}, bf16[128,1152]{1,0:T(8,128)(2,1)S(1)}, f32[128,1152]{1,0:T(8,128)S(1)},...) custom-call(s32[1]{0:T(128)} %bitcast.place, bf16[256,1152]{1,0:T(8,128)(2,1)S(1)} %all_gather.12.mine, ...), custom_call_target="tpu_custom_call" | custom-call | tf_op jit(solution)/shard_map/pallas_call | solution.py:166
  52.4 1.9 %collective-permute-start.6 = (bf16[128,1152]{1,0:T(8,128)(2,1)S(1)}, bf16[128,1152]{1,0:T(8,128)(2,1)S(1)}, u32[]{:S(2)}, u32[]{:S(2)}) collective-permute-start(bf16[128,1152]{1,0:T(8,128)(2,1)S(1)} %get-tuple-element.52), channel_id=1, source_target_pairs={{0,256},{1,257},{2,258},{3,259},{4,260},{5,261},{6,262},{7,263},{8... | collective-permute-start | bytes 884744 | tf_op jit(solution)/shard_map/ppermute | solution.py:230
  54.3 5.1 %collective-permute-start.7 = (bf16[128,1152]{1,0:T(8,128)(2,1)S(1)}, bf16[128,1152]{1,0:T(8,128)(2,1)S(1)}, u32[]{:S(2)}, u32[]{:S(2)}) collective-permute-start(bf16[128,1152]{1,0:T(8,128)(2,1)S(1)} %get-tuple-element.53), channel_id=1, source_target_pairs={{0,128},{1,129},{2,130},{3,131},{4,132},{5,133},{6,134},{7,135},{8... | collective-permute-start | bytes 884744 | tf_op jit(solution)/shard_map/ppermute | solution.py:231
  59.4 3.1 %all_gather.15.gathered = bf16[288,1152]{1,0:T(8,128)(2,1)S(1)} all-gather(bf16[144,1152]{1,0:T(8,128)(2,1)S(1)} %get-tuple-element.46), channel_id=1, replica_groups=mesh['yl'=4,'c'=2,'x'=4,'z'=8,'yh'=2] {'c'}, dimensions={0}, use_global_device_ids=true | all-gather | bytes 995328 | tf_op jit(solution)/shard_map/all_gather | solution.py:204
  62.6 0.1 convert_add_fusion
  62.6 10.8 %collective-permute-done.5.home = bf16[144,1152]{1,0:T(8,128)(2,1)S(1)} collective-permute-done((bf16[144,1152]{1,0:T(8,128)(2,1)S(1)}, bf16[144,1152]{1,0:T(8,128)(2,1)S(1)}, u32[]{:S(2)}, u32[]{:S(2)}) %collective-permute-start.5) | collective-permute-done | bytes 331808 | tf_op jit(solution)/shard_map/ppermute | solution.py:226
  73.5 0.9 %shard_map.72 = (f32[128,1152]{1,0:T(8,128)}, f32[1,128]{1,0:T(1,128)}) custom-call(s32[1]{0:T(128)} %bitcast.place, f32[128,1152]{1,0:T(8,128)S(1)} %get-tuple-element.44.keep, f32[1,128]{1,0:T(1,128)S(1)} %get-tuple-element.45.keep_loss, bf16[288,1152]{1,0:T(8,128)(2,1)S(1)} %all_gather.15.gathered, bf16[144,1152]{1,0:T(8,128)(2,1)S(1)} %collective-permute-done.5.home), custom_call_target="tpu_custom_call" | custom-call | tf_op jit(solution)/shard_map/pallas_call | solution.py:166
  74.4 0.9 %add_add_fusion = f32[128,1152]{1,0:T(8,128)} fusion(f32[128,1152]{1,0:T(8,128)S(1)} %convert_add_fusion, bf16[128,1152]{1,0:T(8,128)(2,1)S(1)} %collective-permute-done.7, bf16[128,1152]{1,0:T(8,128)(2,1)S(1)} %collective-permute-done.6), kind=kLoop, calls=%fused_computation | loop fusion | flops 589824 | bytes 1769472 | tf_op jit(solution)/shard_map/add | solution.py:239
  (7 shorter events, 0.0 us)
Async XLA Ops:
  0.6 31.3 %collective-permute-start.2 = (bf16[128,1152]{1,0:T(8,128)(2,1)}, bf16[128,1152]{1,0:T(8,128)(2,1)S(1)}, u32[]{:S(2)}, u32[]{:S(2)}) collective-permute-start(bf16[128,1152]{1,0:T(8,128)(2,1)} %own.7), channel_id=1, source_target_pairs={{0,128},{1,129},{2,130},{3,131},{4,132},{5,133},{6,134},{7,135},{8... | collective-permute-start | bytes 884744 | tf_op jit(solution)/shard_map/ppermute | solution.py:206
  4.7 27.2 %collective-permute-start.1 = (bf16[128,1152]{1,0:T(8,128)(2,1)}, bf16[128,1152]{1,0:T(8,128)(2,1)S(1)}, u32[]{:S(2)}, u32[]{:S(2)}) collective-permute-start(bf16[128,1152]{1,0:T(8,128)(2,1)} %own.7), channel_id=1, source_target_pairs={{0,384},{1,385},{2,386},{3,387},{4,388},{5,389},{6,390},{7,391},{8... | collective-permute-start | bytes 884744 | tf_op jit(solution)/shard_map/ppermute | solution.py:206
  8.8 27.8 %collective-permute-start = (bf16[128,1152]{1,0:T(8,128)(2,1)}, bf16[128,1152]{1,0:T(8,128)(2,1)S(1)}, u32[]{:S(2)}, u32[]{:S(2)}) collective-permute-start(bf16[128,1152]{1,0:T(8,128)(2,1)} %param.4), channel_id=1, source_target_pairs={{0,447},{1,384},{2,385},{3,386},{4,387},{5,388},{6,389},{7,390},{8... | collective-permute-start | bytes 884744 | tf_op jit(solution)/shard_map/ppermute | solution.py:207
  24.1 20.5 %collective-permute-start.3 = (bf16[128,1152]{1,0:T(8,128)(2,1)}, bf16[128,1152]{1,0:T(8,128)(2,1)S(1)}, u32[]{:S(2)}, u32[]{:S(2)}) collective-permute-start(bf16[128,1152]{1,0:T(8,128)(2,1)} %own.7), channel_id=1, source_target_pairs={{0,256},{1,257},{2,258},{3,259},{4,260},{5,261},{6,262},{7,263},{8... | collective-permute-start | bytes 884744 | tf_op jit(solution)/shard_map/ppermute | solution.py:206
  28.2 3.7 %copy-start = (bf16[128,1152]{1,0:T(8,128)(2,1)S(1)}, bf16[128,1152]{1,0:T(8,128)(2,1)}, u32[]{:S(2)}) copy-start(bf16[128,1152]{1,0:T(8,128)(2,1)} %own.7) | copy-start | bytes 884740
  41.4 21.1 %collective-permute-start.4 = (bf16[128,1152]{1,0:T(8,128)(2,1)S(1)}, bf16[128,1152]{1,0:T(8,128)(2,1)S(1)}, u32[]{:S(2)}, u32[]{:S(2)}) collective-permute-start(bf16[128,1152]{1,0:T(8,128)(2,1)S(1)} %get-tuple-element.43), channel_id=1, source_target_pairs={{0,384},{1,385},{2,386},{3,387},{4,388},{5,389},{6,390},{7,391},{8... | collective-permute-start | bytes 884744 | tf_op jit(solution)/shard_map/ppermute | solution.py:218
  49.2 24.3 %collective-permute-start.5 = (bf16[144,1152]{1,0:T(8,128)(2,1)S(1)}, bf16[144,1152]{1,0:T(8,128)(2,1)S(1)}, u32[]{:S(2)}, u32[]{:S(2)}) collective-permute-start(bf16[144,1152]{1,0:T(8,128)(2,1)S(1)} %shard_map.70.after), channel_id=1, source_target_pairs={{447,0},{384,1},{385,2},{386,3},{387,4},{388,5},{389,6},{390,7},{3... | collective-permute-start | bytes 995336 | tf_op jit(solution)/shard_map/ppermute | solution.py:226
  52.4 22.0 %collective-permute-start.6 = (bf16[128,1152]{1,0:T(8,128)(2,1)S(1)}, bf16[128,1152]{1,0:T(8,128)(2,1)S(1)}, u32[]{:S(2)}, u32[]{:S(2)}) collective-permute-start(bf16[128,1152]{1,0:T(8,128)(2,1)S(1)} %get-tuple-element.52), channel_id=1, source_target_pairs={{0,256},{1,257},{2,258},{3,259},{4,260},{5,261},{6,262},{7,263},{8... | collective-permute-start | bytes 884744 | tf_op jit(solution)/shard_map/ppermute | solution.py:230
  54.3 20.1 %collective-permute-start.7 = (bf16[128,1152]{1,0:T(8,128)(2,1)S(1)}, bf16[128,1152]{1,0:T(8,128)(2,1)S(1)}, u32[]{:S(2)}, u32[]{:S(2)}) collective-permute-start(bf16[128,1152]{1,0:T(8,128)(2,1)S(1)} %get-tuple-element.53), channel_id=1, source_target_pairs={{0,128},{1,129},{2,130},{3,131},{4,132},{5,133},{6,134},{7,135},{8... | collective-permute-start | bytes 884744 | tf_op jit(solution)/shard_map/ppermute | solution.py:231

commit v4 on v3

--- a/solution.py
+++ b/solution.py
@@ -26,9 +26,9 @@
 
     def fn(yl, c, x, z, yh):
         if yh == 1:
-            return nyl - 1 - yl, c, x, z, 0
+            return yl ^ 2, c, x, z, 0
         k = (x * nz + z - 1) % (nx * nz)
-        return nyl - 1 - yl, c, k // nz, k % nz, 1
+        return yl ^ 2, c, k // nz, k % nz, 1
 
     return pairs(sizes, fn)
 
@@ -58,8 +58,8 @@
         bundle[m * rows : (m + 1) * rows, :] = block[...]
 
 
-def own_kernel(place, factors, mine, own, cross, near, slopes, loss, bundle):
-    lay((own, cross, near), bundle)
+def own_kernel(place, factors, mine, own, cross, slopes, loss, bundle):
+    lay((own, cross), bundle)
     rows = own.shape[0]
 
     def positive(shape):
@@ -102,12 +102,12 @@
 
 def visit_kernel(
     place, factors, mine, theirs, own, cross, far, near, first_slopes, first_loss, my_loss,
-    slopes, far_slopes, loss, keep, keep_loss, give, total, first, second, their_loss,
+    slopes, last_slopes, loss, keep, keep_loss, give, total, first, second, their_loss,
 ):
     lay((own, cross), first)
     lay((far, near), second)
     slopes_and_loss(None, factors, theirs, second, slopes, their_loss)
-    slopes_and_loss(None, factors, mine, far, far_slopes, loss)
+    slopes_and_loss(None, factors, mine, second, last_slopes, loss)
     loss[...] += my_loss[...]
     total[...] = contract(first_slopes[...], first[...], ((0,), (0,))) + contract(
         slopes[...], second[...], ((0,), (0,))
@@ -116,8 +116,8 @@
 
 
 def rest_kernel(
-    place, mine, theirs, own, cross, far, near, my_slopes, far_slopes, first_slopes, slopes, loss, after,
-    own_grad, far_grad, near_grad, keep, keep_loss, give, total, bundle,
+    place, mine, theirs, own, cross, far, near, my_slopes, last_slopes, first_slopes, slopes, loss, after,
+    own_grad, far_grad, near_grad, keep, keep_loss, give, total, first, second,
 ):
     rows = own.shape[0]
 
@@ -125,11 +125,12 @@
         return contract(of_mine, mine[...], ((1,), (0,))) + contract(of_theirs, theirs[...], ((1,), (0,)))
 
     own_grad[...] = text_gradient(my_slopes[:rows, :], first_slopes[:rows, :])
-    far_grad[...] = text_gradient(far_slopes[...], slopes[:rows, :]).astype(BF)
-    near_grad[...] = text_gradient(my_slopes[2 * rows :, :], slopes[rows:, :]).astype(BF)
-    lay((own, cross, near), bundle)
-    total[...] = contract(my_slopes[...], bundle[...], ((0,), (0,))) + contract(
-        far_slopes[...], far[...], ((0,), (0,))
+    far_grad[...] = text_gradient(last_slopes[:rows, :], slopes[:rows, :]).astype(BF)
+    near_grad[...] = text_gradient(last_slopes[rows:, :], slopes[rows:, :]).astype(BF)
+    lay((own, cross), first)
+    lay((far, near), second)
+    total[...] = contract(my_slopes[...], first[...], ((0,), (0,))) + contract(
+        last_slopes[...], second[...], ((0,), (0,))
     )
     split_cores(place[0], total, loss[...], keep, keep_loss, give)
 
@@ -207,8 +208,8 @@
         visitors = lax.ppermute(images, AXES, go)
         mine = both_cores(images)
 
-        my_slopes, my_loss = call(own_kernel, 2, [slope(3), line], [bundle(3)])(
-            place, factors, mine, texts, cross, near
+        my_slopes, my_loss = call(own_kernel, 2, [slope(2), line], [bundle(2)])(
+            place, factors, mine, texts, cross
         )
         visitors, my_slopes = bar((visitors, my_slopes))
         theirs = both_cores(visitors)
@@ -216,17 +217,17 @@
             factors, mine, theirs, texts, cross, my_slopes
         )
         cross_home = lax.ppermute(cross_grad, AXES, across[3])
-        slopes1, far_slopes, loss, keep_v, keep_loss_v, give_v = call(
+        slopes1, last_slopes, loss, keep_v, keep_loss_v, give_v = call(
             visit_kernel,
             2,
-            [slope(2), slope(1), line, wide, short, message],
+            [slope(2), slope(2), line, wide, short, message],
             [total, bundle(2), bundle(2), pltpu.VMEM((1, 2 * rows), F32)],
         )(place, factors, mine, theirs, texts, cross, far, near, slopes0, loss0, my_loss)
         (sent,) = call(visitor_kernel, 1, [message])(place, keep_v, keep_loss_v, both_cores(give_v))
         home = lax.ppermute(sent, AXES, back)
         own_grad, far_grad, near_grad, keep, keep_loss, give = call(
-            rest_kernel, 1, [wide, block, block, wide, short, message], [total, bundle(3)]
-        )(place, mine, theirs, texts, cross, far, near, my_slopes, far_slopes, slopes0, slopes1, loss, sent)
+            rest_kernel, 1, [wide, block, block, wide, short, message], [total, bundle(2), bundle(2)]
+        )(place, mine, theirs, texts, cross, far, near, my_slopes, last_slopes, slopes0, slopes1, loss, sent)
         far_home = lax.ppermute(far_grad, AXES, across[2])
         near_home = lax.ppermute(near_grad, AXES, across[1])
 

time: 75.7 us -> 72.7 us (0.960)
  the two profiles are of different devices: /device:TPU:1 before, /device:TPU:8 now
where the time goes in v4:
time: 72.7 us; the launch traced here: 72.3 us
  starting transfers between devices  39.3 us (54%)
  waiting for transfers between devices  13.7 us (19%)
  blocking collectives  9.35 us (13%)
  Pallas kernels  6.91 us (10%)
  between operations  2.05 us (3%)
  other arithmetic  1.03 us (1%)
    ppermute x1, starting transfers between devices, shards(): visitors = lax.ppermute(images, AXES, go)  17.3 us
    ppermute x1, waiting for transfers between devices, shards(): home = lax.ppermute(sent, AXES, back)  13.6 us
    all_gather x4, blocking collectives, both_cores(): return lax.all_gather(array, 'c', axis=0, tiled=True)  9.35 us
    ppermute x3, starting transfers between devices, shards(): cross, near, far = (lax.ppermute(texts, AXES, across[m]) for m in (3, 1, 2))  8.77 us
    pallas_call x6, Pallas kernels, run(): pl.pallas_call(kernel, out_shape=outs, in_specs=[SMEM] * scalars + [VMEM]...  6.91 us
    ppermute x1, starting transfers between devices, shards(): far_home = lax.ppermute(far_grad, AXES, across[2])  4.19 us
    ppermute x1, starting transfers between devices, shards(): cross_home = lax.ppermute(cross_grad, AXES, across[3])  3.92 us
    ppermute x1, starting transfers between devices, shards(): near_home = lax.ppermute(near_grad, AXES, across[1])  2.91 us
  transfers between devices with their start and end apart: 8, of which 1 were waited for; matrix products, arithmetic and copies ran while one was open for 0% of the time, Pallas kernels for 10%

profile of v4, /device:TPU:8, one launch (start us, length us, event | category | flops | bytes accessed | tf_op | source)
XLA Modules:
  0.0 72.3 jit_solution(5201417454387542855)
XLA Ops:
  0.6 3.5 %collective-permute-start.1 = (bf16[128,1152]{1,0:T(8,128)(2,1)}, bf16[128,1152]{1,0:T(8,128)(2,1)S(1)}, u32[]{:S(2)}, u32[]{:S(2)}) collective-permute-start(bf16[128,1152]{1,0:T(8,128)(2,1)} %own.7), channel_id=1, source_target_pairs={{0,384},{1,385},{2,386},{3,387},{4,388},{5,389},{6,390},{7,391},{8... | collective-permute-start | bytes 884744 | tf_op jit(solution)/shard_map/ppermute | solution.py:207
  4.1 17.3 %collective-permute-start = (bf16[128,1152]{1,0:T(8,128)(2,1)}, bf16[128,1152]{1,0:T(8,128)(2,1)S(1)}, u32[]{:S(2)}, u32[]{:S(2)}) collective-permute-start(bf16[128,1152]{1,0:T(8,128)(2,1)} %param.4), channel_id=1, source_target_pairs={{0,319},{1,256},{2,257},{3,258},{4,259},{5,260},{6,261},{7,262},{8... | collective-permute-start | bytes 884744 | tf_op jit(solution)/shard_map/ppermute | solution.py:208
  21.4 1.9 %collective-permute-start.3 = (bf16[128,1152]{1,0:T(8,128)(2,1)}, bf16[128,1152]{1,0:T(8,128)(2,1)S(1)}, u32[]{:S(2)}, u32[]{:S(2)}) collective-permute-start(bf16[128,1152]{1,0:T(8,128)(2,1)} %own.7), channel_id=1, source_target_pairs={{0,128},{1,129},{2,130},{3,131},{4,132},{5,133},{6,134},{7,135},{8... | collective-permute-start | bytes 884744 | tf_op jit(solution)/shard_map/ppermute | solution.py:207
  23.3 3.4 %collective-permute-start.2 = (bf16[128,1152]{1,0:T(8,128)(2,1)}, bf16[128,1152]{1,0:T(8,128)(2,1)S(1)}, u32[]{:S(2)}, u32[]{:S(2)}) collective-permute-start(bf16[128,1152]{1,0:T(8,128)(2,1)} %own.7), channel_id=1, source_target_pairs={{0,256},{1,257},{2,258},{3,259},{4,260},{5,261},{6,262},{7,263},{8... | collective-permute-start | bytes 884744 | tf_op jit(solution)/shard_map/ppermute | solution.py:207
  28.0 0.1 pad_maximum_fusion.factors
  28.1 2.6 %all_gather.12.mine = bf16[256,1152]{1,0:T(8,128)(2,1)S(1)} all-gather(bf16[128,1152]{1,0:T(8,128)(2,1)} %param.4), channel_id=1, replica_groups=mesh['yl'=4,'c'=2,'x'=4,'z'=8,'yh'=2] {'c'}, dimensions={0}, use_global_device_ids=true | all-gather | bytes 884736 | tf_op jit(solution)/shard_map/all_gather | solution.py:205
  30.6 0.0 collective-permute-done.1.cross
  30.7 1.1 %shard_map.67 = (bf16[256,256]{1,0:T(8,128)(2,1)S(1)}, f32[1,256]{1,0:T(1,128)S(1)}) custom-call(s32[1]{0:T(128)} %bitcast.place, f32[2]{0:T(128)S(1)} %pad_maximum_fusion.factors, bf16[256,1152]{1,0:T(8,128)(2,1)S(1)} %all_gather.12.mine, bf16[128,1152]{1,0:T(8,128)(2,1)S(1)} %copy-done, bf16[128,1152]{1,0:T(8,128)(2,1)S(1)} %collective-permute-done.1.cross), custom_call_target="tpu_custom_call" | custom-call | tf_op jit(solution)/shard_map/pallas_call | solution.py:167
  31.8 2.2 %all_gather.13.theirs = bf16[256,1152]{1,0:T(8,128)(2,1)S(1)} all-gather(bf16[128,1152]{1,0:T(8,128)(2,1)S(1)} %collective-permute-done), channel_id=1, replica_groups=mesh['yl'=4,'c'=2,'x'=4,'z'=8,'yh'=2] {'c'}, dimensions={0}, use_global_device_ids=true | all-gather | bytes 884736 | tf_op jit(solution)/shard_map/all_gather | solution.py:205
  34.0 1.6 %shard_map.68 = (bf16[256,256]{1,0:T(8,128)(2,1)S(1)}, f32[1,256]{1,0:T(1,128)S(1)}, bf16[128,1152]{1,0:T(8,128)(2,1)S(1)}) custom-call(f32[2]{0:T(128)S(1)} %pad_maximum_fusion.factors, bf16[256,1152]{1,0:T(8,128)(2,1)S(1)} %all_gather.12.mine, bf16[256,1152]{1,0:T(8,128)(2,1)S(1)} %all_gather.13.theirs, bf16[128,1152]{1,0:T(8,128)(2,1)S(1)} %copy-done, ...), custom_call_target="tpu_custom_call" | custom-call | tf_op jit(solution)/shard_map/pallas_call | solution.py:167
  35.6 3.9 %collective-permute-start.4 = (bf16[128,1152]{1,0:T(8,128)(2,1)S(1)}, bf16[128,1152]{1,0:T(8,128)(2,1)S(1)}, u32[]{:S(2)}, u32[]{:S(2)}) collective-permute-start(bf16[128,1152]{1,0:T(8,128)(2,1)S(1)} %get-tuple-element.43), channel_id=1, source_target_pairs={{0,384},{1,385},{2,386},{3,387},{4,388},{5,389},{6,390},{7,391},{8... | collective-permute-start | bytes 884744 | tf_op jit(solution)/shard_map/ppermute | solution.py:219
  39.6 0.0 collective-permute-done.2.far
  39.6 2.0 %shard_map.69 = (bf16[256,256]{1,0:T(8,128)(2,1)S(1)}, bf16[256,256]{1,0:T(8,128)(2,1)S(1)}, f32[1,256]{1,0:T(1,128)S(1)}, f32[128,1152]{1,0:T(8,128)S(1)}, f32[...) custom-call(s32[1]{0:T(128)} %bitcast.place, f32[2]{0:T(128)S(1)} %pad_maximum_fusion.factors, ...), custom_call_target="tpu_custom_call" | custom-call | tf_op jit(solution)/shard_map/pallas_call | solution.py:167
  41.6 2.3 %all_gather.14.gathered = bf16[288,1152]{1,0:T(8,128)(2,1)S(1)} all-gather(bf16[144,1152]{1,0:T(8,128)(2,1)S(1)} %get-tuple-element.40), channel_id=1, replica_groups=mesh['yl'=4,'c'=2,'x'=4,'z'=8,'yh'=2] {'c'}, dimensions={0}, use_global_device_ids=true | all-gather | bytes 995328 | tf_op jit(solution)/shard_map/all_gather | solution.py:205
  43.9 0.1 shard_map.70.after
  44.0 2.2 %collective-permute-start.5 = (bf16[144,1152]{1,0:T(8,128)(2,1)S(1)}, bf16[144,1152]{1,0:T(8,128)(2,1)S(1)}, u32[]{:S(2)}, u32[]{:S(2)}) collective-permute-start(bf16[144,1152]{1,0:T(8,128)(2,1)S(1)} %shard_map.70.after), channel_id=1, source_target_pairs={{319,0},{256,1},{257,2},{258,3},{259,4},{260,5},{261,6},{262,7},{2... | collective-permute-start | bytes 995336 | tf_op jit(solution)/shard_map/ppermute | solution.py:227
  46.2 1.1 %shard_map.71 = (f32[128,1152]{1,0:T(8,128)S(1)}, bf16[128,1152]{1,0:T(8,128)(2,1)S(1)}, bf16[128,1152]{1,0:T(8,128)(2,1)S(1)}, f32[128,1152]{1,0:T(8,128)S(1)},...) custom-call(s32[1]{0:T(128)} %bitcast.place, bf16[256,1152]{1,0:T(8,128)(2,1)S(1)} %all_gather.12.mine, ...), custom_call_target="tpu_custom_call" | custom-call | tf_op jit(solution)/shard_map/pallas_call | solution.py:167
  47.4 4.2 %collective-permute-start.6 = (bf16[128,1152]{1,0:T(8,128)(2,1)S(1)}, bf16[128,1152]{1,0:T(8,128)(2,1)S(1)}, u32[]{:S(2)}, u32[]{:S(2)}) collective-permute-start(bf16[128,1152]{1,0:T(8,128)(2,1)S(1)} %get-tuple-element.52), channel_id=1, source_target_pairs={{0,256},{1,257},{2,258},{3,259},{4,260},{5,261},{6,262},{7,263},{8... | collective-permute-start | bytes 884744 | tf_op jit(solution)/shard_map/ppermute | solution.py:231
  51.6 2.9 %collective-permute-start.7 = (bf16[128,1152]{1,0:T(8,128)(2,1)S(1)}, bf16[128,1152]{1,0:T(8,128)(2,1)S(1)}, u32[]{:S(2)}, u32[]{:S(2)}) collective-permute-start(bf16[128,1152]{1,0:T(8,128)(2,1)S(1)} %get-tuple-element.53), channel_id=1, source_target_pairs={{0,128},{1,129},{2,130},{3,131},{4,132},{5,133},{6,134},{7,135},{8... | collective-permute-start | bytes 884744 | tf_op jit(solution)/shard_map/ppermute | solution.py:232
  54.5 2.3 %all_gather.15.gathered = bf16[288,1152]{1,0:T(8,128)(2,1)S(1)} all-gather(bf16[144,1152]{1,0:T(8,128)(2,1)S(1)} %get-tuple-element.46), channel_id=1, replica_groups=mesh['yl'=4,'c'=2,'x'=4,'z'=8,'yh'=2] {'c'}, dimensions={0}, use_global_device_ids=true | all-gather | bytes 995328 | tf_op jit(solution)/shard_map/all_gather | solution.py:205
  56.8 0.1 convert_add_fusion
  56.8 13.6 %collective-permute-done.5.home = bf16[144,1152]{1,0:T(8,128)(2,1)S(1)} collective-permute-done((bf16[144,1152]{1,0:T(8,128)(2,1)S(1)}, bf16[144,1152]{1,0:T(8,128)(2,1)S(1)}, u32[]{:S(2)}, u32[]{:S(2)}) %collective-permute-start.5) | collective-permute-done | bytes 331808 | tf_op jit(solution)/shard_map/ppermute | solution.py:227
  70.5 0.9 %shard_map.72 = (f32[128,1152]{1,0:T(8,128)}, f32[1,128]{1,0:T(1,128)}) custom-call(s32[1]{0:T(128)} %bitcast.place, f32[128,1152]{1,0:T(8,128)S(1)} %get-tuple-element.44.keep, f32[1,128]{1,0:T(1,128)S(1)} %get-tuple-element.45.keep_loss, bf16[288,1152]{1,0:T(8,128)(2,1)S(1)} %all_gather.15.gathered, bf16[144,1152]{1,0:T(8,128)(2,1)S(1)} %collective-permute-done.5.home), custom_call_target="tpu_custom_call" | custom-call | tf_op jit(solution)/shard_map/pallas_call | solution.py:167
  71.4 0.9 %add_add_fusion = f32[128,1152]{1,0:T(8,128)} fusion(f32[128,1152]{1,0:T(8,128)S(1)} %convert_add_fusion, bf16[128,1152]{1,0:T(8,128)(2,1)S(1)} %collective-permute-done.7, bf16[128,1152]{1,0:T(8,128)(2,1)S(1)} %collective-permute-done.6), kind=kLoop, calls=%fused_computation | loop fusion | flops 589824 | bytes 1769472 | tf_op jit(solution)/shard_map/add | solution.py:240
  (7 shorter events, 0.0 us)
Async XLA Ops:
  0.6 30.0 %collective-permute-start.1 = (bf16[128,1152]{1,0:T(8,128)(2,1)}, bf16[128,1152]{1,0:T(8,128)(2,1)S(1)}, u32[]{:S(2)}, u32[]{:S(2)}) collective-permute-start(bf16[128,1152]{1,0:T(8,128)(2,1)} %own.7), channel_id=1, source_target_pairs={{0,384},{1,385},{2,386},{3,387},{4,388},{5,389},{6,390},{7,391},{8... | collective-permute-start | bytes 884744 | tf_op jit(solution)/shard_map/ppermute | solution.py:207
  4.1 27.6 %collective-permute-start = (bf16[128,1152]{1,0:T(8,128)(2,1)}, bf16[128,1152]{1,0:T(8,128)(2,1)S(1)}, u32[]{:S(2)}, u32[]{:S(2)}) collective-permute-start(bf16[128,1152]{1,0:T(8,128)(2,1)} %param.4), channel_id=1, source_target_pairs={{0,319},{1,256},{2,257},{3,258},{4,259},{5,260},{6,261},{7,262},{8... | collective-permute-start | bytes 884744 | tf_op jit(solution)/shard_map/ppermute | solution.py:208
  21.4 18.2 %collective-permute-start.3 = (bf16[128,1152]{1,0:T(8,128)(2,1)}, bf16[128,1152]{1,0:T(8,128)(2,1)S(1)}, u32[]{:S(2)}, u32[]{:S(2)}) collective-permute-start(bf16[128,1152]{1,0:T(8,128)(2,1)} %own.7), channel_id=1, source_target_pairs={{0,128},{1,129},{2,130},{3,131},{4,132},{5,133},{6,134},{7,135},{8... | collective-permute-start | bytes 884744 | tf_op jit(solution)/shard_map/ppermute | solution.py:207
  23.3 16.2 %collective-permute-start.2 = (bf16[128,1152]{1,0:T(8,128)(2,1)}, bf16[128,1152]{1,0:T(8,128)(2,1)S(1)}, u32[]{:S(2)}, u32[]{:S(2)}) collective-permute-start(bf16[128,1152]{1,0:T(8,128)(2,1)} %own.7), channel_id=1, source_target_pairs={{0,256},{1,257},{2,258},{3,259},{4,260},{5,261},{6,262},{7,263},{8... | collective-permute-start | bytes 884744 | tf_op jit(solution)/shard_map/ppermute | solution.py:207
  28.1 2.6 %copy-start = (bf16[128,1152]{1,0:T(8,128)(2,1)S(1)}, bf16[128,1152]{1,0:T(8,128)(2,1)}, u32[]{:S(2)}) copy-start(bf16[128,1152]{1,0:T(8,128)(2,1)} %own.7) | copy-start | bytes 884740
  35.6 21.1 %collective-permute-start.4 = (bf16[128,1152]{1,0:T(8,128)(2,1)S(1)}, bf16[128,1152]{1,0:T(8,128)(2,1)S(1)}, u32[]{:S(2)}, u32[]{:S(2)}) collective-permute-start(bf16[128,1152]{1,0:T(8,128)(2,1)S(1)} %get-tuple-element.43), channel_id=1, source_target_pairs={{0,384},{1,385},{2,386},{3,387},{4,388},{5,389},{6,390},{7,391},{8... | collective-permute-start | bytes 884744 | tf_op jit(solution)/shard_map/ppermute | solution.py:219
  44.0 26.5 %collective-permute-start.5 = (bf16[144,1152]{1,0:T(8,128)(2,1)S(1)}, bf16[144,1152]{1,0:T(8,128)(2,1)S(1)}, u32[]{:S(2)}, u32[]{:S(2)}) collective-permute-start(bf16[144,1152]{1,0:T(8,128)(2,1)S(1)} %shard_map.70.after), channel_id=1, source_target_pairs={{319,0},{256,1},{257,2},{258,3},{259,4},{260,5},{261,6},{262,7},{2... | collective-permute-start | bytes 995336 | tf_op jit(solution)/shard_map/ppermute | solution.py:227
  47.4 24.0 %collective-permute-start.6 = (bf16[128,1152]{1,0:T(8,128)(2,1)S(1)}, bf16[128,1152]{1,0:T(8,128)(2,1)S(1)}, u32[]{:S(2)}, u32[]{:S(2)}) collective-permute-start(bf16[128,1152]{1,0:T(8,128)(2,1)S(1)} %get-tuple-element.52), channel_id=1, source_target_pairs={{0,256},{1,257},{2,258},{3,259},{4,260},{5,261},{6,262},{7,263},{8... | collective-permute-start | bytes 884744 | tf_op jit(solution)/shard_map/ppermute | solution.py:231
  51.6 19.8 %collective-permute-start.7 = (bf16[128,1152]{1,0:T(8,128)(2,1)S(1)}, bf16[128,1152]{1,0:T(8,128)(2,1)S(1)}, u32[]{:S(2)}, u32[]{:S(2)}) collective-permute-start(bf16[128,1152]{1,0:T(8,128)(2,1)S(1)} %get-tuple-element.53), channel_id=1, source_target_pairs={{0,128},{1,129},{2,130},{3,131},{4,132},{5,133},{6,134},{7,135},{8... | collective-permute-start | bytes 884744 | tf_op jit(solution)/shard_map/ppermute | solution.py:232

commit v5 on v4

--- a/solution.py
+++ b/solution.py
@@ -115,18 +115,21 @@
     split_cores(place[0], total, their_loss[...] + first_loss[...], keep, keep_loss, give)
 
 
+def text_kernel(mine, theirs, last_slopes, slopes, after, far_grad, near_grad):
+    rows = far_grad.shape[0]
+    grad = contract(last_slopes[...], mine[...], ((1,), (0,))) + contract(slopes[...], theirs[...], ((1,), (0,)))
+    far_grad[...] = grad[:rows, :].astype(BF)
+    near_grad[...] = grad[rows:, :].astype(BF)
+
+
 def rest_kernel(
-    place, mine, theirs, own, cross, far, near, my_slopes, last_slopes, first_slopes, slopes, loss, after,
-    own_grad, far_grad, near_grad, keep, keep_loss, give, total, first, second,
+    place, mine, theirs, own, cross, far, near, my_slopes, last_slopes, first_slopes, loss, after,
+    own_grad, keep, keep_loss, give, total, first, second,
 ):
     rows = own.shape[0]
-
-    def text_gradient(of_mine, of_theirs):
-        return contract(of_mine, mine[...], ((1,), (0,))) + contract(of_theirs, theirs[...], ((1,), (0,)))
-
-    own_grad[...] = text_gradient(my_slopes[:rows, :], first_slopes[:rows, :])
-    far_grad[...] = text_gradient(last_slopes[:rows, :], slopes[:rows, :]).astype(BF)
-    near_grad[...] = text_gradient(last_slopes[rows:, :], slopes[rows:, :]).astype(BF)
+    own_grad[...] = contract(my_slopes[:rows, :], mine[...], ((1,), (0,))) + contract(
+        first_slopes[:rows, :], theirs[...], ((1,), (0,))
+    )
     lay((own, cross), first)
     lay((far, near), second)
     total[...] = contract(my_slopes[...], first[...], ((0,), (0,))) + contract(
@@ -225,11 +228,12 @@
         )(place, factors, mine, theirs, texts, cross, far, near, slopes0, loss0, my_loss)
         (sent,) = call(visitor_kernel, 1, [message])(place, keep_v, keep_loss_v, both_cores(give_v))
         home = lax.ppermute(sent, AXES, back)
-        own_grad, far_grad, near_grad, keep, keep_loss, give = call(
-            rest_kernel, 1, [wide, block, block, wide, short, message], [total, bundle(2), bundle(2)]
-        )(place, mine, theirs, texts, cross, far, near, my_slopes, last_slopes, slopes0, slopes1, loss, sent)
+        far_grad, near_grad = call(text_kernel, 0, [block, block])(mine, theirs, last_slopes, slopes1, sent)
         far_home = lax.ppermute(far_grad, AXES, across[2])
         near_home = lax.ppermute(near_grad, AXES, across[1])
+        own_grad, keep, keep_loss, give = call(
+            rest_kernel, 1, [wide, wide, short, message], [total, bundle(2), bundle(2)]
+        )(place, mine, theirs, texts, cross, far, near, my_slopes, last_slopes, slopes0, loss, near_grad)
 
         two = own_grad + cross_home.astype(F32)
         keep, two = bar((keep, two))

time: 72.7 us -> 72.7 us (level)
    pallas_call x6 -> x7, Pallas kernels: 6.91 us -> 7.03 us  [run(): pl.pallas_call(kernel, out_shape=outs, in_specs=[SMEM] * scalars + [VMEM]...]
where the time goes in v5:
time: 72.7 us; the launch traced here: 72.3 us
  starting transfers between devices  39.3 us (54%)
  waiting for transfers between devices  13.5 us (19%)
  blocking collectives  9.35 us (13%)
  Pallas kernels  7.03 us (10%)
  between operations  2.05 us (3%)
  other arithmetic  1.02 us (1%)
    ppermute x1, starting transfers between devices, shards(): visitors = lax.ppermute(images, AXES, go)  17.3 us
    ppermute x1, waiting for transfers between devices, shards(): home = lax.ppermute(sent, AXES, back)  13.5 us
    all_gather x4, blocking collectives, both_cores(): return lax.all_gather(array, 'c', axis=0, tiled=True)  9.35 us
    ppermute x3, starting transfers between devices, shards(): cross, near, far = (lax.ppermute(texts, AXES, across[m]) for m in (3, 1, 2))  8.77 us
    pallas_call x7, Pallas kernels, run(): pl.pallas_call(kernel, out_shape=outs, in_specs=[SMEM] * scalars + [VMEM]...  7.03 us
    ppermute x1, starting transfers between devices, shards(): far_home = lax.ppermute(far_grad, AXES, across[2])  4.19 us
    ppermute x1, starting transfers between devices, shards(): cross_home = lax.ppermute(cross_grad, AXES, across[3])  3.93 us
    ppermute x1, starting transfers between devices, shards(): near_home = lax.ppermute(near_grad, AXES, across[1])  2.91 us
  transfers between devices with their start and end apart: 8, of which 1 were waited for; matrix products, arithmetic and copies ran while one was open for 0% of the time, Pallas kernels for 10%

profile of v5, /device:TPU:8, one launch (start us, length us, event | category | flops | bytes accessed | tf_op | source)
XLA Modules:
  0.0 72.3 jit_solution(11332472117848255452)
XLA Ops:
  0.6 3.5 %collective-permute-start.1 = (bf16[128,1152]{1,0:T(8,128)(2,1)}, bf16[128,1152]{1,0:T(8,128)(2,1)S(1)}, u32[]{:S(2)}, u32[]{:S(2)}) collective-permute-start(bf16[128,1152]{1,0:T(8,128)(2,1)} %own.7), channel_id=1, source_target_pairs={{0,384},{1,385},{2,386},{3,387},{4,388},{5,389},{6,390},{7,391},{8... | collective-permute-start | bytes 884744 | tf_op jit(solution)/shard_map/ppermute | solution.py:210
  4.1 17.3 %collective-permute-start = (bf16[128,1152]{1,0:T(8,128)(2,1)}, bf16[128,1152]{1,0:T(8,128)(2,1)S(1)}, u32[]{:S(2)}, u32[]{:S(2)}) collective-permute-start(bf16[128,1152]{1,0:T(8,128)(2,1)} %param.4), channel_id=1, source_target_pairs={{0,319},{1,256},{2,257},{3,258},{4,259},{5,260},{6,261},{7,262},{8... | collective-permute-start | bytes 884744 | tf_op jit(solution)/shard_map/ppermute | solution.py:211
  21.4 1.9 %collective-permute-start.3 = (bf16[128,1152]{1,0:T(8,128)(2,1)}, bf16[128,1152]{1,0:T(8,128)(2,1)S(1)}, u32[]{:S(2)}, u32[]{:S(2)}) collective-permute-start(bf16[128,1152]{1,0:T(8,128)(2,1)} %own.7), channel_id=1, source_target_pairs={{0,128},{1,129},{2,130},{3,131},{4,132},{5,133},{6,134},{7,135},{8... | collective-permute-start | bytes 884744 | tf_op jit(solution)/shard_map/ppermute | solution.py:210
  23.3 3.4 %collective-permute-start.2 = (bf16[128,1152]{1,0:T(8,128)(2,1)}, bf16[128,1152]{1,0:T(8,128)(2,1)S(1)}, u32[]{:S(2)}, u32[]{:S(2)}) collective-permute-start(bf16[128,1152]{1,0:T(8,128)(2,1)} %own.7), channel_id=1, source_target_pairs={{0,256},{1,257},{2,258},{3,259},{4,260},{5,261},{6,262},{7,263},{8... | collective-permute-start | bytes 884744 | tf_op jit(solution)/shard_map/ppermute | solution.py:210
  28.0 0.1 pad_maximum_fusion.factors
  28.1 2.6 %all_gather.12.mine = bf16[256,1152]{1,0:T(8,128)(2,1)S(1)} all-gather(bf16[128,1152]{1,0:T(8,128)(2,1)} %param.4), channel_id=1, replica_groups=mesh['yl'=4,'c'=2,'x'=4,'z'=8,'yh'=2] {'c'}, dimensions={0}, use_global_device_ids=true | all-gather | bytes 884736 | tf_op jit(solution)/shard_map/all_gather | solution.py:208
  30.6 0.0 collective-permute-done.1.cross
  30.7 1.1 %shard_map.67 = (bf16[256,256]{1,0:T(8,128)(2,1)S(1)}, f32[1,256]{1,0:T(1,128)S(1)}) custom-call(s32[1]{0:T(128)} %bitcast.place, f32[2]{0:T(128)S(1)} %pad_maximum_fusion.factors, bf16[256,1152]{1,0:T(8,128)(2,1)S(1)} %all_gather.12.mine, bf16[128,1152]{1,0:T(8,128)(2,1)S(1)} %copy-done, bf16[128,1152]{1,0:T(8,128)(2,1)S(1)} %collective-permute-done.1.cross), custom_call_target="tpu_custom_call" | custom-call | tf_op jit(solution)/shard_map/pallas_call | solution.py:170
  31.8 2.2 %all_gather.13.theirs = bf16[256,1152]{1,0:T(8,128)(2,1)S(1)} all-gather(bf16[128,1152]{1,0:T(8,128)(2,1)S(1)} %collective-permute-done), channel_id=1, replica_groups=mesh['yl'=4,'c'=2,'x'=4,'z'=8,'yh'=2] {'c'}, dimensions={0}, use_global_device_ids=true | all-gather | bytes 884736 | tf_op jit(solution)/shard_map/all_gather | solution.py:208
  34.0 1.6 %shard_map.68 = (bf16[256,256]{1,0:T(8,128)(2,1)S(1)}, f32[1,256]{1,0:T(1,128)S(1)}, bf16[128,1152]{1,0:T(8,128)(2,1)S(1)}) custom-call(f32[2]{0:T(128)S(1)} %pad_maximum_fusion.factors, bf16[256,1152]{1,0:T(8,128)(2,1)S(1)} %all_gather.12.mine, bf16[256,1152]{1,0:T(8,128)(2,1)S(1)} %all_gather.13.theirs, bf16[128,1152]{1,0:T(8,128)(2,1)S(1)} %copy-done, ...), custom_call_target="tpu_custom_call" | custom-call | tf_op jit(solution)/shard_map/pallas_call | solution.py:170
  35.6 3.9 %collective-permute-start.4 = (bf16[128,1152]{1,0:T(8,128)(2,1)S(1)}, bf16[128,1152]{1,0:T(8,128)(2,1)S(1)}, u32[]{:S(2)}, u32[]{:S(2)}) collective-permute-start(bf16[128,1152]{1,0:T(8,128)(2,1)S(1)} %get-tuple-element.44), channel_id=1, source_target_pairs={{0,384},{1,385},{2,386},{3,387},{4,388},{5,389},{6,390},{7,391},{8... | collective-permute-start | bytes 884744 | tf_op jit(solution)/shard_map/ppermute | solution.py:222
  39.6 2.0 %shard_map.69 = (bf16[256,256]{1,0:T(8,128)(2,1)S(1)}, bf16[256,256]{1,0:T(8,128)(2,1)S(1)}, f32[1,256]{1,0:T(1,128)S(1)}, f32[128,1152]{1,0:T(8,128)S(1)}, f32[...) custom-call(s32[1]{0:T(128)} %bitcast.place, f32[2]{0:T(128)S(1)} %pad_maximum_fusion.factors, ...), custom_call_target="tpu_custom_call" | custom-call | tf_op jit(solution)/shard_map/pallas_call | solution.py:170
  41.6 2.3 %all_gather.14.gathered = bf16[288,1152]{1,0:T(8,128)(2,1)S(1)} all-gather(bf16[144,1152]{1,0:T(8,128)(2,1)S(1)} %get-tuple-element.40), channel_id=1, replica_groups=mesh['yl'=4,'c'=2,'x'=4,'z'=8,'yh'=2] {'c'}, dimensions={0}, use_global_device_ids=true | all-gather | bytes 995328 | tf_op jit(solution)/shard_map/all_gather | solution.py:208
  43.9 0.1 shard_map.70.after
  44.0 2.2 %collective-permute-start.5 = (bf16[144,1152]{1,0:T(8,128)(2,1)S(1)}, bf16[144,1152]{1,0:T(8,128)(2,1)S(1)}, u32[]{:S(2)}, u32[]{:S(2)}) collective-permute-start(bf16[144,1152]{1,0:T(8,128)(2,1)S(1)} %shard_map.70.after), channel_id=1, source_target_pairs={{319,0},{256,1},{257,2},{258,3},{259,4},{260,5},{261,6},{262,7},{2... | collective-permute-start | bytes 995336 | tf_op jit(solution)/shard_map/ppermute | solution.py:230
  46.2 0.5 shard_map.71
  46.7 4.2 %collective-permute-start.6 = (bf16[128,1152]{1,0:T(8,128)(2,1)S(1)}, bf16[128,1152]{1,0:T(8,128)(2,1)S(1)}, u32[]{:S(2)}, u32[]{:S(2)}) collective-permute-start(bf16[128,1152]{1,0:T(8,128)(2,1)S(1)} %get-tuple-element.53), channel_id=1, source_target_pairs={{0,256},{1,257},{2,258},{3,259},{4,260},{5,261},{6,262},{7,263},{8... | collective-permute-start | bytes 884744 | tf_op jit(solution)/shard_map/ppermute | solution.py:232
  50.9 2.9 %collective-permute-start.7 = (bf16[128,1152]{1,0:T(8,128)(2,1)S(1)}, bf16[128,1152]{1,0:T(8,128)(2,1)S(1)}, u32[]{:S(2)}, u32[]{:S(2)}) collective-permute-start(bf16[128,1152]{1,0:T(8,128)(2,1)S(1)} %get-tuple-element.41.after), channel_id=1, source_target_pairs={{0,128},{1,129},{2,130},{3,131},{4,132},{5,133},{6,134},{7,135},{8... | collective-permute-start | bytes 884744 | tf_op jit(solution)/shard_map/ppermute | solution.py:233
  53.9 0.8 %shard_map.72 = (f32[128,1152]{1,0:T(8,128)S(1)}, f32[128,1152]{1,0:T(8,128)S(1)}, f32[1,128]{1,0:T(1,128)S(1)}, bf16[144,1152]{1,0:T(8,128)(2,1)S(1)}) custom-call(s32[1]{0:T(128)} %bitcast.place, bf16[256,1152]{1,0:T(8,128)(2,1)S(1)} %all_gather.12.mine, bf16[256,1152]{1,0:T(8,128)(2,1)S(1)} %all_gather.13.theirs, bf16[128,1152]{1,0:T(8,128)(2,1)S(1)} %copy-done, ...), custom_call_target="tpu_custom_call" | custom-call | tf_op jit(solution)/shard_map/pallas_call | solution.py:170
  54.6 2.3 %all_gather.15.gathered = bf16[288,1152]{1,0:T(8,128)(2,1)S(1)} all-gather(bf16[144,1152]{1,0:T(8,128)(2,1)S(1)} %get-tuple-element.47), channel_id=1, replica_groups=mesh['yl'=4,'c'=2,'x'=4,'z'=8,'yh'=2] {'c'}, dimensions={0}, use_global_device_ids=true | all-gather | bytes 995328 | tf_op jit(solution)/shard_map/all_gather | solution.py:208
  56.9 0.1 convert_add_fusion
  57.0 13.5 %collective-permute-done.5.home = bf16[144,1152]{1,0:T(8,128)(2,1)S(1)} collective-permute-done((bf16[144,1152]{1,0:T(8,128)(2,1)S(1)}, bf16[144,1152]{1,0:T(8,128)(2,1)S(1)}, u32[]{:S(2)}, u32[]{:S(2)}) %collective-permute-start.5) | collective-permute-done | bytes 331808 | tf_op jit(solution)/shard_map/ppermute | solution.py:230
  70.5 0.9 %shard_map.73 = (f32[128,1152]{1,0:T(8,128)}, f32[1,128]{1,0:T(1,128)}) custom-call(s32[1]{0:T(128)} %bitcast.place, f32[128,1152]{1,0:T(8,128)S(1)} %get-tuple-element.45.keep, f32[1,128]{1,0:T(1,128)S(1)} %get-tuple-element.46.keep_loss, bf16[288,1152]{1,0:T(8,128)(2,1)S(1)} %all_gather.15.gathered, bf16[144,1152]{1,0:T(8,128)(2,1)S(1)} %collective-permute-done.5.home), custom_call_target="tpu_custom_call" | custom-call | tf_op jit(solution)/shard_map/pallas_call | solution.py:170
  71.4 0.9 %add_add_fusion = f32[128,1152]{1,0:T(8,128)} fusion(f32[128,1152]{1,0:T(8,128)S(1)} %convert_add_fusion, bf16[128,1152]{1,0:T(8,128)(2,1)S(1)} %collective-permute-done.7, bf16[128,1152]{1,0:T(8,128)(2,1)S(1)} %collective-permute-done.6), kind=kLoop, calls=%fused_computation | loop fusion | flops 589824 | bytes 1769472 | tf_op jit(solution)/shard_map/add | solution.py:244
  (8 shorter events, 0.0 us)
Async XLA Ops:
  0.6 30.0 %collective-permute-start.1 = (bf16[128,1152]{1,0:T(8,128)(2,1)}, bf16[128,1152]{1,0:T(8,128)(2,1)S(1)}, u32[]{:S(2)}, u32[]{:S(2)}) collective-permute-start(bf16[128,1152]{1,0:T(8,128)(2,1)} %own.7), channel_id=1, source_target_pairs={{0,384},{1,385},{2,386},{3,387},{4,388},{5,389},{6,390},{7,391},{8... | collective-permute-start | bytes 884744 | tf_op jit(solution)/shard_map/ppermute | solution.py:210
  4.1 27.6 %collective-permute-start = (bf16[128,1152]{1,0:T(8,128)(2,1)}, bf16[128,1152]{1,0:T(8,128)(2,1)S(1)}, u32[]{:S(2)}, u32[]{:S(2)}) collective-permute-start(bf16[128,1152]{1,0:T(8,128)(2,1)} %param.4), channel_id=1, source_target_pairs={{0,319},{1,256},{2,257},{3,258},{4,259},{5,260},{6,261},{7,262},{8... | collective-permute-start | bytes 884744 | tf_op jit(solution)/shard_map/ppermute | solution.py:211
  21.4 18.2 %collective-permute-start.3 = (bf16[128,1152]{1,0:T(8,128)(2,1)}, bf16[128,1152]{1,0:T(8,128)(2,1)S(1)}, u32[]{:S(2)}, u32[]{:S(2)}) collective-permute-start(bf16[128,1152]{1,0:T(8,128)(2,1)} %own.7), channel_id=1, source_target_pairs={{0,128},{1,129},{2,130},{3,131},{4,132},{5,133},{6,134},{7,135},{8... | collective-permute-start | bytes 884744 | tf_op jit(solution)/shard_map/ppermute | solution.py:210
  23.3 16.2 %collective-permute-start.2 = (bf16[128,1152]{1,0:T(8,128)(2,1)}, bf16[128,1152]{1,0:T(8,128)(2,1)S(1)}, u32[]{:S(2)}, u32[]{:S(2)}) collective-permute-start(bf16[128,1152]{1,0:T(8,128)(2,1)} %own.7), channel_id=1, source_target_pairs={{0,256},{1,257},{2,258},{3,259},{4,260},{5,261},{6,262},{7,263},{8... | collective-permute-start | bytes 884744 | tf_op jit(solution)/shard_map/ppermute | solution.py:210
  28.1 2.6 %copy-start = (bf16[128,1152]{1,0:T(8,128)(2,1)S(1)}, bf16[128,1152]{1,0:T(8,128)(2,1)}, u32[]{:S(2)}) copy-start(bf16[128,1152]{1,0:T(8,128)(2,1)} %own.7) | copy-start | bytes 884740
  35.6 21.3 %collective-permute-start.4 = (bf16[128,1152]{1,0:T(8,128)(2,1)S(1)}, bf16[128,1152]{1,0:T(8,128)(2,1)S(1)}, u32[]{:S(2)}, u32[]{:S(2)}) collective-permute-start(bf16[128,1152]{1,0:T(8,128)(2,1)S(1)} %get-tuple-element.44), channel_id=1, source_target_pairs={{0,384},{1,385},{2,386},{3,387},{4,388},{5,389},{6,390},{7,391},{8... | collective-permute-start | bytes 884744 | tf_op jit(solution)/shard_map/ppermute | solution.py:222
  44.0 26.5 %collective-permute-start.5 = (bf16[144,1152]{1,0:T(8,128)(2,1)S(1)}, bf16[144,1152]{1,0:T(8,128)(2,1)S(1)}, u32[]{:S(2)}, u32[]{:S(2)}) collective-permute-start(bf16[144,1152]{1,0:T(8,128)(2,1)S(1)} %shard_map.70.after), channel_id=1, source_target_pairs={{319,0},{256,1},{257,2},{258,3},{259,4},{260,5},{261,6},{262,7},{2... | collective-permute-start | bytes 995336 | tf_op jit(solution)/shard_map/ppermute | solution.py:230
  46.7 24.7 %collective-permute-start.6 = (bf16[128,1152]{1,0:T(8,128)(2,1)S(1)}, bf16[128,1152]{1,0:T(8,128)(2,1)S(1)}, u32[]{:S(2)}, u32[]{:S(2)}) collective-permute-start(bf16[128,1152]{1,0:T(8,128)(2,1)S(1)} %get-tuple-element.53), channel_id=1, source_target_pairs={{0,256},{1,257},{2,258},{3,259},{4,260},{5,261},{6,262},{7,263},{8... | collective-permute-start | bytes 884744 | tf_op jit(solution)/shard_map/ppermute | solution.py:232
  50.9 20.5 %collective-permute-start.7 = (bf16[128,1152]{1,0:T(8,128)(2,1)S(1)}, bf16[128,1152]{1,0:T(8,128)(2,1)S(1)}, u32[]{:S(2)}, u32[]{:S(2)}) collective-permute-start(bf16[128,1152]{1,0:T(8,128)(2,1)S(1)} %get-tuple-element.41.after), channel_id=1, source_target_pairs={{0,128},{1,129},{2,130},{3,131},{4,132},{5,133},{6,134},{7,135},{8... | collective-permute-start | bytes 884744 | tf_op jit(solution)/shard_map/ppermute | solution.py:233
